TPU v7x, 32 devices: a whole 2x2x4 slice. The times are simulated.
32 devices in a mesh: tm: 8 (over z, y), mark: 4 (over x, core).
Axes of the slice: x: 2, y: 2, z: 4, core: 2. Of those that a mesh axis runs over, the one named last changes fastest.
Arguments:
- event_marks: int32 [32768], P('tm'), may hold values from 0 to 8191
- event_gaps: int32 [32768], P('tm'), may hold values from 1 to 65536, as said below
- excite: bfloat16 [512, 8192], P('mark'), may hold values from 0 to 0.59765625
- source: bfloat16 [512, 8192], P('mark'), may hold values from 0 to 0.59765625
- base_rate: float32 [8192], replicated, may hold values from 0.05 to 0.5
- weights: float32 [8], replicated, may hold values from 0.2 to 2
- decay_rates: float32 [8], replicated, may hold values from 1.0172526041666667e-06 to 0.06666667
Outputs:
- grad_excite: float32 [512, 8192], P('mark', 'tm')
- grad_source: float32 [512, 8192], P('mark', 'tm')
- grad_base: float32 [8192], P('tm')
Inputs may be any that keep to these rules, and one draw needn't show every extreme that they name: `event_gaps`: ticks since the previous event, the first counted from time 0.
All inputs are finite; a program needn't handle non-finite values.
Results may differ from a plain program's by a relative error of at most 0.0003.
Values sent between devices are 32-bit elements; how exact they have to be, the bound alone decides.
A program may use at most 64 MiB of HBM per device.

v0:
```python
import functools

import jax
import jax.numpy as jnp
from jax import lax
from jax.experimental import pallas as pl
from jax.experimental.pallas import tpu as pltpu
from jax.sharding import PartitionSpec as P

F32 = jnp.float32
BF16 = jnp.bfloat16
B = 128
HIGH = lax.Precision.HIGHEST
VMEM = pl.BlockSpec(memory_space=pltpu.VMEM)
SMEM = pl.BlockSpec(memory_space=pltpu.SMEM)
NT = (((1,), (1,)), ((), ()))


def iota(shape, axis):
    return lax.broadcasted_iota(jnp.int32, shape, axis)


def split(a):
    high = a.astype(BF16)
    return high, (a - high.astype(F32)).astype(BF16)


def dot(a, b):
    return jnp.dot(a, b, preferred_element_type=F32)


def two_term(a, b):
    high, low = split(a)
    n = a.shape[0]
    both = dot(jnp.concatenate([high.astype(F32), low.astype(F32)], 0).astype(BF16), b)
    return both[:n] + both[n:]


def down(ref, count, width=B):
    row = iota((count, width), 0)
    out = jnp.zeros((count, width), F32)
    for k in range(count):
        out = jnp.where(row == k, ref[k], out)
    return out


def across(ref, count, copies):
    lane = iota((1, B), 1)
    out = jnp.zeros((1, B), F32)
    for k in range(count):
        hit = (lane < copies * count) & (lax.rem(lane, count) == k)
        out = jnp.where(hit, ref[k], out)
    return out


def columns(u):
    blocks = u.shape[0]
    return jnp.concatenate([u, jnp.zeros((B - blocks, B), F32)], 0).T


def state_rows(state):
    high, low = split(state)
    high, low = high.astype(F32), low.astype(F32)
    fill = jnp.zeros((B - 3 * state.shape[0], state.shape[1]), F32)
    return jnp.concatenate([high, low, high, fill], 0).astype(BF16)


def state_lanes(a, count):
    high, low = split(a)
    lane = iota(a.shape, 1)
    return jnp.where(lane < 2 * count, high.astype(F32), low.astype(F32)).astype(BF16)


def gather_kernel(
    count, marks, decay, gaps, src, exc, srows, xrows, u_out, sums, device, xtot, tab_s, tab_x
):
    events, width = srows.shape
    blocks = events // B

    def turn(c, total):
        s = pl.ds(pl.multiple_of(c * B, B), B)
        tab_s[s, :] = src[:, s].astype(F32).T
        t = exc[:, s].astype(F32).T
        tab_x[s, :] = t
        return total + jnp.sum(t.reshape(B // 8, 8, width), axis=0)

    total = lax.fori_loop(0, src.shape[1] // B, turn, jnp.zeros((8, width), F32))
    xtot[...] = jnp.broadcast_to(jnp.sum(total, axis=0, keepdims=True), (8, width))

    def fetch(g, _):
        for j in range(16):
            e = g * 16 + j
            m = marks[e]
            srows[pl.ds(e, 1), :] = tab_s[pl.ds(m, 1), :]
            xrows[pl.ds(e, 1), :] = tab_x[pl.ds(m, 1), :]
        return 0

    lax.fori_loop(0, events // 16, fetch, 0)
    upper = (iota((B, B), 0) <= iota((B, B), 1)).astype(F32)
    u = jnp.dot(gaps[...].astype(F32), upper, precision=HIGH, preferred_element_type=F32)
    u_out[...] = u
    d, dw = down(decay, count), down(decay, count, width)
    state = jnp.zeros((count, width), F32)
    duration = jnp.zeros((1, 1), F32)
    for b in range(blocks):
        ub = u[b : b + 1, :]
        length = ub[:, B - 1 :]
        values = srows[b * B : (b + 1) * B, :].astype(BF16)
        part = two_term(d * jnp.exp(-d * (length - ub)), values)
        sums[b * count : (b + 1) * count, :] = part
        state = state * jnp.exp(-dw * length) + part
        duration = duration + length
    device[0:count, :] = state
    device[count:, :] = jnp.broadcast_to(duration, (8, width))


def inside_kernel(count, weights, decay, u_ref, marks, base, srows, sym, inside, lanes, base_e):
    blocks = u_ref.shape[0]
    u = u_ref[...]
    ut = columns(u)
    wide_d, wide_w = across(decay, count, 3), across(weights, count, 3)
    earlier = iota((B, B), 0) > iota((B, B), 1)
    bh, bl = split(base[...])
    base2 = jnp.concatenate([bh.astype(F32), bl.astype(F32)], 0).T.astype(BF16)
    groups = base.shape[0]
    for b in range(blocks):
        col = ut[:, b : b + 1]
        row = u[b : b + 1, :]
        apart = jnp.abs(col - row)
        g = jnp.zeros((B, B), F32)
        for k in range(count):
            g = g + (weights[k] * decay[k]) * jnp.exp(-decay[k] * apart)
        s = slice(b * B, (b + 1) * B)
        sym[s, :] = g
        high, low = split(jnp.where(earlier, g, 0.0))
        values = srows[s, :].astype(BF16)
        inside[s, :] = dot(high, values) + dot(low, values)
        lanes[s, :] = state_lanes(wide_w * jnp.exp(-wide_d * col), count)
        m = marks[b : b + 1, :]
        hi, lo = m // B, lax.rem(m, B)
        pick = (lax.rem(iota((2 * groups, B), 0), groups) == hi).astype(BF16)
        found = dot(base2, pick)
        base_e[b : b + 1, :] = jnp.sum(
            jnp.where(iota((B, B), 0) == lo, found, 0.0), axis=0, keepdims=True
        )


def forward_kernel(
    count, rank, weights, decay, place, u_ref, summaries, sums, lanes, inside, srows, xrows,
    excitation, partial, remain, misc,
):
    blocks = u_ref.shape[0]
    peers = summaries.shape[0]
    me = place[0]
    u = u_ref[...]
    width = srows.shape[1]
    d, w, dw = down(decay, count), down(weights, count), down(decay, count, width)
    state = jnp.zeros((count, width), F32)
    after = jnp.zeros((1, 1), F32)
    end = jnp.zeros((1, 1), F32)
    for r in range(peers):
        length = summaries[r, count : count + 1, 0:1]
        state = jnp.where(
            r < me, state * jnp.exp(-dw * length) + summaries[r, 0:count, :], state
        )
        after = after + jnp.where(r > me, length, 0.0)
        end = end + length
    ones = jnp.ones((8, width), BF16)
    for b in range(blocks):
        s = slice(b * B, (b + 1) * B)
        length = u[b : b + 1, B - 1 :]
        value = inside[s, :] + dot(lanes[s, :], state_rows(state))
        excitation[s, :] = value
        product = value * xrows[s, :]
        high, low = split(product)
        total = lax.dot_general(ones, high, NT, preferred_element_type=F32)
        total = total + lax.dot_general(ones, low, NT, preferred_element_type=F32)
        partial[b : b + 1, :] = total[0:1, :] * (1.0 / rank)
        state = state * jnp.exp(-dw * length) + sums[b * count : (b + 1) * count, :]
    comp = jnp.zeros((8, width), F32)
    for b in reversed(range(blocks)):
        s = slice(b * B, (b + 1) * B)
        ub = u[b : b + 1, :]
        length = ub[:, B - 1 :]
        left = jnp.sum(w * (1.0 - jnp.exp(-d * (length - ub + after))), axis=0, keepdims=True)
        remain[b : b + 1, :] = left
        comp = comp + two_term(jnp.broadcast_to(left, (8, B)), srows[s, :].astype(BF16))
        after = after + length
    misc[0:8, :] = comp
    misc[8:16, :] = jnp.broadcast_to(end, (8, width))


def reverse_kernel(count, decay, u_ref, marks, base_e, total, xrows, comp, inverse, sums, device, base_sum):
    blocks = u_ref.shape[0]
    u = u_ref[...]
    inv = 1.0 / (base_e[...] + sum(total[r] for r in range(total.shape[0])))
    inverse[...] = inv
    width = xrows.shape[1]
    d, dw = down(decay, count), down(decay, count, width)
    groups = base_sum.shape[0]
    pending = jnp.zeros((count, width), F32)
    both = jnp.zeros((2 * groups, B), F32)
    for b in reversed(range(blocks)):
        s = slice(b * B, (b + 1) * B)
        ub = u[b : b + 1, :]
        length = ub[:, B - 1 :]
        ib = inv[b : b + 1, :]
        part = two_term(d * jnp.exp(-d * ub) * ib, xrows[s, :].astype(BF16))
        sums[b * count : (b + 1) * count, :] = part
        pending = pending * jnp.exp(-dw * length) + part
        m = marks[b : b + 1, :]
        hi, lo = m // B, lax.rem(m, B)
        ih = ib.astype(BF16).astype(F32)
        spread = jnp.concatenate([jnp.broadcast_to(ih, (groups, B)), jnp.broadcast_to(ib - ih, (groups, B))], 0)
        left = jnp.where(lax.rem(iota((2 * groups, B), 0), groups) == hi, spread, 0.0).astype(BF16)
        right = (iota((B, B), 0) == lo).astype(BF16)
        both = both + lax.dot_general(left, right, NT, preferred_element_type=F32)
    base_sum[...] = both[:groups] + both[groups:]
    device[0:count, :] = pending
    device[count:, :] = comp[0:8, :]


def scatter(marks, values, out):
    def group(g, _):
        e = g * 4
        m = [marks[e + j] for j in range(4)]
        add = [values[pl.ds(e + j, 1), :] for j in range(4)]
        old = [out[pl.ds(r, 1), :] for r in m]
        for j in range(4):
            new = old[j] + add[j]
            for i in range(j):
                new = new + jnp.where(m[i] == m[j], add[i], 0.0)
            out[pl.ds(m[j], 1), :] = new
        return 0

    lax.fori_loop(0, values.shape[0] // 4, group, 0, unroll=4)


def clear(out):
    def zero(i, _):
        out[pl.ds(pl.multiple_of(i * 8, 8), 8), :] = jnp.zeros((8, out.shape[1]), F32)
        return 0

    lax.fori_loop(0, out.shape[0] // 8, zero, 0, unroll=8)


def scatter_excite_kernel(marks, inverse, excitation, out, values):
    blocks = inverse.shape[0]
    clear(out)
    cols = columns(inverse[...])
    for b in range(blocks):
        s = slice(b * B, (b + 1) * B)
        values[s, :] = excitation[s, :] * cols[:, b : b + 1]
    scatter(marks, values, out)


def call(kernel, ins, outs, scratch=(), flops=10**8):
    return pl.pallas_call(
        kernel,
        out_shape=[jax.ShapeDtypeStruct(s, t) for s, t in outs],
        in_specs=list(ins),
        out_specs=[VMEM] * len(outs),
        scratch_shapes=list(scratch),
        compiler_params=pltpu.CompilerParams(vmem_limit_bytes=40 * 2**20),
        cost_estimate=pl.CostEstimate(flops=flops, bytes_accessed=4 * 2**20, transcendentals=10**6),
    )


def exchange_kernel(axis, n, spread, *refs):
    k = len(spread)
    ins, outs, send, recv = refs[:k], refs[k : 2 * k], refs[2 * k], refs[2 * k + 1]
    me = lax.axis_index(axis)
    peers = [lax.rem(me + i, n) for i in range(1, n)]
    barrier = pltpu.get_barrier_semaphore()
    for p in peers:
        pl.semaphore_signal(barrier, inc=1, device_id={axis: p}, device_id_type=pl.DeviceIdType.MESH)
    pl.semaphore_wait(barrier, n - 1)
    copies = []
    for a in range(k):
        for i, p in enumerate(peers):
            copy = pltpu.make_async_remote_copy(
                src_ref=ins[a].at[p] if spread[a] else ins[a],
                dst_ref=outs[a].at[me],
                send_sem=send.at[a, i],
                recv_sem=recv.at[a, i],
                device_id={axis: p},
                device_id_type=pl.DeviceIdType.MESH,
            )
            copy.start()
            copies.append(copy)
    for a in range(k):
        outs[a][me] = ins[a][me] if spread[a] else ins[a][...]
    for copy in copies:
        copy.wait()


def exchange(arrays, axis, spread, collective):
    n = lax.axis_size(axis)
    k = len(arrays)
    shapes = [a.shape if s else (n,) + a.shape for a, s in zip(arrays, spread)]
    return pl.pallas_call(
        functools.partial(exchange_kernel, axis, n, spread),
        out_shape=[jax.ShapeDtypeStruct(s, F32) for s in shapes],
        in_specs=[VMEM] * k,
        out_specs=[VMEM] * k,
        scratch_shapes=[pltpu.SemaphoreType.DMA((k, n - 1))] * 2,
        compiler_params=pltpu.CompilerParams(collective_id=collective, has_side_effects=True),
    )(*arrays)


def feedback_values(count, me, weights, decay, u_ref, inverse, remain, xtot, summaries, back, sums, sym, xrows, types, pair):
    blocks = u_ref.shape[0]
    peers = summaries.shape[0]
    u = u_ref[...]
    width = xrows.shape[1]
    dw = down(decay, count, width)
    wide_d, wide_w = across(decay, count, 3), across(weights, count, 3)
    pending = jnp.zeros((count, width), F32)
    for r in reversed(range(peers)):
        length = summaries[r, count : count + 1, 0:1]
        pending = jnp.where(r > me, pending * jnp.exp(-dw * length) + back[r, 0:count, :], pending)
    ut, rem_t = columns(u), columns(remain[...])
    share = xtot[0:1, :] * (1.0 / types)
    later = iota((B, B), 0) < iota((B, B), 1)
    for b in reversed(range(blocks)):
        s = slice(b * B, (b + 1) * B)
        length = u[b : b + 1, B - 1 :]
        high, low = split(jnp.where(later, sym[s, :] * inverse[b : b + 1, :], 0.0))
        x = xrows[s, :].astype(BF16)
        lanes = state_lanes(wide_w * jnp.exp(-wide_d * (length - ut[:, b : b + 1])), count)
        value = dot(high, x) + dot(low, x) + dot(lanes, state_rows(pending))
        value = value - rem_t[:, b : b + 1] * share
        high, low = split(value)
        pair[s, :] = jnp.concatenate([high.astype(F32), low.astype(F32)], 1).astype(BF16)
        pending = pending * jnp.exp(-dw * length) + sums[b * count : (b + 1) * count, :]


def ring_kernel(
    n, count, weights, decay, x0, marks, u_ref, inverse, remain, xtot, summaries, back, sums, sym, xrows,
    out0, out1, x1, pair, hot, slots, send, recv,
):
    xs, outs = (x0, x1), (out0, out1)
    per, width = out0.shape
    half = per // 2
    tile = hot.shape[0]
    me = lax.axis_index("tm")
    odd = lax.rem(me, 2)
    at = lax.div(me, 2) + odd * (lax.div(2 * n - 1 - me, 2) - lax.div(me, 2))

    def member(place):
        c = lax.rem(place + 2 * n, n)
        return 2 * c + lax.div(c, n // 2) * (2 * n - 1 - 4 * c)

    towards = (member(at + 1), member(at - 1))
    barrier = pltpu.get_barrier_semaphore()
    for p in towards:
        pl.semaphore_signal(barrier, inc=1, device_id={"tm": p}, device_id_type=pl.DeviceIdType.MESH)
    pl.semaphore_wait(barrier, 2)

    def rows(j, step):
        way = j % 2
        block = member(at + 1 + step) if way else member(at - 1 - step)
        return pl.ds(pl.multiple_of(block * per + way * half, 8), half)

    def copy(j, step, source):
        return pltpu.make_async_remote_copy(
            src_ref=source,
            dst_ref=slots.at[j, step],
            send_sem=send.at[j, step],
            recv_sem=recv.at[j, step],
            device_id={"tm": towards[j % 2]},
            device_id_type=pl.DeviceIdType.MESH,
        )

    def begin(chains):
        for j in chains:
            copy(j, 0, xs[j // 2].at[rows(j, 0)]).start()

    def step(s, chains):
        for j in chains:
            held = slots.at[j, s - 1]
            copy(j, s - 1, held).wait_recv()
            held[...] += xs[j // 2][rows(j, s), :]
            copy(j, s, held).start()

    def finish(chains):
        for j in chains:
            copy(j, n - 2, slots.at[j, n - 2]).wait_recv()
            start = (j % 2) * half
            own = pl.ds(pl.multiple_of(me * per + start, 8), half)
            outs[j // 2][start : start + half, :] = slots[j, n - 2] + xs[j // 2][own, :]

    def chunk(block):
        def part(t, _):
            first = block * per + t * tile
            kind = iota((tile, B), 0) + first
            for b in range(marks.shape[0]):
                hot[:, b * B : (b + 1) * B] = (kind == marks[b : b + 1, :]).astype(BF16)
            both = dot(hot[...], pair[...])
            x1[pl.ds(pl.multiple_of(first, 8), tile), :] = both[:, :width] + both[:, width:]
            return 0

        lax.fori_loop(0, per // tile, part, 0)

    begin((0, 1))
    feedback_values(
        count, me, weights, decay, u_ref, inverse, remain, xtot, summaries, back, sums, sym, xrows, x0.shape[0], pair
    )

    def excite_step(s, _):
        step(s, (0, 1))
        i = s - 1
        away = lax.div(i, 2) + 1
        chunk(member(at + away * (2 * lax.rem(i, 2) - 1)))
        return 0

    def two_steps(p, _):
        lax.fori_loop(2 * p + 1, 2 * p + 3, excite_step, 0)
        step(p, (2, 3))
        return 0

    lax.fori_loop(1, 3, excite_step, 0)
    begin((2, 3))
    lax.fori_loop(1, n // 2 - 1, two_steps, 0)

    def rest(i, _):
        chunk(member(at + i * (n // 2)))
        return 0

    lax.fori_loop(0, 2, rest, 0)
    finish((0, 1))

    def source_step(s, _):
        step(s, (2, 3))
        return 0

    lax.fori_loop(n // 2 - 1, n - 1, source_step, 0)
    finish((2, 3))

    def sent(s, _):
        for j in range(4):
            copy(j, s, slots.at[j, s]).wait_send()
        return 0

    lax.fori_loop(0, n - 1, sent, 0)


def ring_sum(count, weights, decay, x0, *rest):
    n = lax.axis_size("tm")
    types, width = x0.shape
    per = types // n
    events = rest[-1].shape[0]
    return pl.pallas_call(
        functools.partial(ring_kernel, n, count),
        out_shape=[jax.ShapeDtypeStruct((per, width), F32)] * 2,
        in_specs=[SMEM] * 2 + [VMEM] * (1 + len(rest)),
        out_specs=[VMEM] * 2,
        scratch_shapes=[
            pltpu.VMEM((types, width), F32),
            pltpu.VMEM((events, 2 * width), BF16),
            pltpu.VMEM((min(256, per), events), BF16),
            pltpu.VMEM((4, n - 1, per // 2, width), F32),
            pltpu.SemaphoreType.DMA((4, n - 1)),
            pltpu.SemaphoreType.DMA((4, n - 1)),
        ],
        compiler_params=pltpu.CompilerParams(
            collective_id=3, has_side_effects=True, vmem_limit_bytes=48 * 2**20
        ),
    )(weights, decay, x0, *rest)


def body(marks, gaps, excite, source, base_rate, weights, decay):
    events = marks.shape[0]
    blocks = events // B
    slices, types = excite.shape
    rank = slices * lax.axis_size("mark")
    peers = lax.axis_size("tm")
    count = decay.shape[0]
    place = lax.axis_index("tm").reshape(1)
    flat = marks.reshape(blocks, B)
    rows = ((events, slices), F32)
    plane = ((blocks, B), F32)
    parts = ((blocks * count, slices), F32)
    packet = ((count + 8, slices), F32)

    srows, xrows, u, sums, device, xtot = call(
        functools.partial(gather_kernel, count),
        [SMEM, SMEM, VMEM, VMEM, VMEM],
        [rows, rows, plane, parts, packet, ((8, slices), F32)],
        [pltpu.VMEM((types, slices), F32)] * 2,
    )(marks, decay, gaps.reshape(blocks, B), source, excite)
    (summaries,) = exchange([device], "tm", [False], 0)
    sym, inside, lanes, base_e = call(
        functools.partial(inside_kernel, count),
        [SMEM, SMEM] + [VMEM] * 4,
        [((events, B), F32), rows, ((events, B), BF16), plane],
        flops=5 * 10**9,
    )(weights, decay, u, flat, base_rate.reshape(types // B, B), srows)
    excitation, partial, remain, misc = call(
        functools.partial(forward_kernel, count, rank),
        [SMEM, SMEM, SMEM] + [VMEM] * 7,
        [rows, plane, plane, ((16, slices), F32)],
    )(weights, decay, place, u, summaries, sums, lanes, inside, srows, xrows)
    (total,) = exchange([partial], "mark", [False], 1)
    inverse, back_sums, back_device, base_sum = call(
        functools.partial(reverse_kernel, count),
        [SMEM] + [VMEM] * 6,
        [plane, parts, packet, ((types // B, B), F32)],
    )(decay, u, flat, base_e, total, xrows, misc)
    back, base_parts = exchange(
        [back_device, base_sum.reshape(peers, types // B // peers, B)], "tm", [False, True], 2
    )
    (excite_term,) = call(
        scatter_excite_kernel,
        [SMEM] + [VMEM] * 2,
        [((types, slices), F32)],
        [pltpu.VMEM((events, slices), F32)],
        flops=10**10,
    )(marks, inverse, excitation)
    excite_part, source_part = ring_sum(
        count, weights, decay, excite_term, flat, u, inverse, remain, xtot, summaries, back, back_sums, sym, xrows
    )
    comp = jnp.sum(back[:, count, :], axis=0)
    base_part = jnp.sum(base_parts, axis=0).reshape(types // peers)

    events_all = events * peers
    factor = types / events_all
    grad_excite = factor * excite_part.T - comp[:, None] / events_all
    grad_base = factor * base_part - misc[8, 0] / events_all
    return grad_excite, factor * source_part.T, grad_base


def solution(mesh):
    return jax.shard_map(
        body,
        mesh=mesh,
        in_specs=(P("tm"), P("tm"), P("mark", None), P("mark", None), P(), P(), P()),
        out_specs=(P("mark", "tm"), P("mark", "tm"), P("tm")),
        check_vma=False,
    )
```

profile of v0, /device:TPU:0, one launch (start us, length us, event | category | flops | bytes accessed | tf_op | source)
XLA Modules:
  0.0 178.8 jit_solution(17179379099519403301)
XLA Ops:
  0.6 1.6 copy-done.1
  2.2 1.6 copy-done.2
  3.8 0.7 copy-done.9
  4.5 0.7 copy-done.13
  5.9 14.1 %shard_map.94 = (f32[4096,128]{1,0:T(8,128)S(1)}, f32[4096,128]{1,0:T(8,128)S(1)}, f32[32,128]{1,0:T(8,128)S(1)}, f32[256,128]{1,0:T(8,128)S(1)}, f32[16,128]{1,0:T(8,128)S(1)}, /*index=5*/f32[8,128]{1,0:T(8,128)S(1)}) custom-call(s32[4096]{0:T(1024)S(1)} %copy-done.9, f32[8]{0:T(128)S(1)} %copy-done.15, s32[32,128]{1,0:T(8,128)S(1)} %bitcast.16, ...), custom_call_target="tpu_custom_call" | custom-call | flops 100000000 | bytes 4194304 | tf_op jit(solution)/shard_map/pallas_call | solution.py:486
  20.0 1.3 copy-done.5
  22.0 10.0 %shard_map.96.summaries = f32[8,16,128]{2,1,0:T(8,128)} custom-call(f32[16,128]{1,0:T(8,128)} %copy-done.18), custom_call_target="tpu_custom_call" | custom-call | tf_op jit(solution)/shard_map/pallas_call | solution.py:301
  32.0 1.6 copy-done.6
  33.6 5.3 %shard_map.95 = (f32[4096,128]{1,0:T(8,128)S(1)}, f32[4096,128]{1,0:T(8,128)S(1)}, bf16[4096,128]{1,0:T(8,128)(2,1)S(1)}, f32[32,128]{1,0:T(8,128)S(1)}) custom-call(f32[8]{0:T(128)S(1)} %copy-done.19, f32[8]{0:T(128)S(1)} %copy-done.16, f32[32,128]{1,0:T(8,128)S(1)} %get-tuple-element.25.u_ref, s32[32,128]{1,0:T(8,128)S(1)} %bitcast.12, ...), custom_call_target="tpu_custom_call" | custom-call | flops 5000000000 | bytes 4194304 | tf_op jit(solution)/shard_map/pallas_call | solution.py:493
  38.9 1.3 copy-done.3
  40.2 4.2 %shard_map.97 = (f32[4096,128]{1,0:T(8,128)S(1)}, f32[32,128]{1,0:T(8,128)S(1)}, f32[32,128]{1,0:T(8,128)S(1)}, f32[16,128]{1,0:T(8,128)S(1)}) custom-call(f32[8]{0:T(128)S(1)} %copy-done.19, f32[8]{0:T(128)S(1)} %copy-done.16, s32[1]{0:T(128)} %bitcast.3.place, f32[32,128]{1,0:T(8,128)S(1)} %get-tuple-element.25.u_ref, f32[8,16,128]{2,1,0:T(8,128)S(1)} %copy-done.7, ...), custom_call_target="tpu_custom_call" | custom-call | flops 100000000 | bytes 4194304 | tf_op jit(solution)/shard_map/pallas_call | solution.py:499
  45.1 1.3 copy-done.20
  47.6 5.1 %shard_map.98.total = f32[4,32,128]{2,1,0:T(8,128)} custom-call(f32[32,128]{1,0:T(8,128)} %copy-done.14), custom_call_target="tpu_custom_call" | custom-call | tf_op jit(solution)/shard_map/pallas_call | solution.py:301
  52.7 0.8 copy-done.8
  53.6 1.7 shard_map.99
  56.5 9.1 %shard_map.101 = (f32[8,16,128]{2,1,0:T(8,128)}, f32[8,8,128]{2,1,0:T(8,128)}) custom-call(f32[16,128]{1,0:T(8,128)} %copy-done.17, f32[8,8,128]{2,1,0:T(8,128)} %bitcast.15), custom_call_target="tpu_custom_call" | custom-call | tf_op jit(solution)/shard_map/pallas_call | solution.py:301
  65.6 0.8 reduce_sum.19
  67.0 0.8 slice_reduce_fusion
  67.8 1.6 copy-done.21
  69.3 13.5 %shard_map.100.x0 = f32[8192,128]{1,0:T(8,128)S(1)} custom-call(s32[4096]{0:T(1024)S(1)} %copy-done.10, f32[32,128]{1,0:T(8,128)S(1)} %get-tuple-element.35.inverse, f32[4096,128]{1,0:T(8,128)S(1)} %copy-done.21), custom_call_target="tpu_custom_call" | custom-call | flops 10000000000 | bytes 4194304 | tf_op jit(solution)/shard_map/pallas_call | solution.py:513
  82.8 1.9 %copy-done = f32[8192,128]{1,0:T(8,128)} copy-done((f32[8192,128]{1,0:T(8,128)}, f32[8192,128]{1,0:T(8,128)S(1)}, u32[]{:S(2)}) %copy-start) | copy-done | bytes 4194328
  84.8 91.9 %shard_map.102 = (f32[1024,128]{1,0:T(8,128)S(1)}, f32[1024,128]{1,0:T(8,128)S(1)}) custom-call(f32[8]{0:T(128)S(1)} %copy-done.19, f32[8]{0:T(128)S(1)} %copy-done.16, f32[8192,128]{1,0:T(8,128)} %copy-done, s32[32,128]{1,0:T(8,128)S(1)} %bitcast.14, f32[32,128]{1,0:T(8,128)S(1)} %get-tuple-element.25.u_ref, f32[32,128]{1,0:T(8,128)S(1)} %get-tuple-element.35.inverse, ...), custom_call_target="tpu_custom_call" | custom-call | tf_op jit(solution)/shard_map/pallas_call | solution.py:453
  176.8 1.0 copy.11
  177.8 1.0 copy.10
  (39 shorter events, 4.3 us)
Async XLA Ops:
  0.6 1.6 copy-start.1
  2.2 1.6 copy-start.2
  3.8 0.7 copy-start.9
  4.5 0.7 copy-start.13
  5.3 0.7 copy-start.15
  5.9 26.1 %copy-start.10 = (s32[4096]{0:T(1024)S(1)}, s32[4096]{0:T(1024)}, u32[]{:S(2)}) copy-start(s32[4096]{0:T(1024)} %marks.3) | copy-start | bytes 49156
  5.9 26.1 %copy-start.16 = (f32[8]{0:T(128)S(1)}, f32[8]{0:T(128)}, u32[]{:S(2)}) copy-start(f32[8]{0:T(128)} %decay.9) | copy-start | bytes 100
  5.9 26.1 %copy-start.19 = (f32[8]{0:T(128)S(1)}, f32[8]{0:T(128)}, u32[]{:S(2)}) copy-start(f32[8]{0:T(128)} %weights.5) | copy-start | bytes 100
  5.9 26.1 %copy-start.22 = (f32[8192]{0:T(1024)S(1)}, f32[8192]{0:T(1024)}, u32[]{:S(2)}) copy-start(f32[8192]{0:T(1024)} %param.11) | copy-start | bytes 98308
  20.0 1.4 copy-start.5
  21.4 0.6 copy-start.18
  32.0 1.6 copy-start.6
  33.6 6.6 %copy-start.7 = (f32[8,16,128]{2,1,0:T(8,128)S(1)}, f32[8,16,128]{2,1,0:T(8,128)}, u32[]{:S(2)}) copy-start(f32[8,16,128]{2,1,0:T(8,128)} %shard_map.96.summaries) | copy-start | bytes 196612
  38.9 1.3 copy-start.3
  44.5 0.6 copy-start.14
  45.1 1.3 copy-start.20
  52.7 0.8 copy-start.8
  55.2 0.6 copy-start.12
  55.9 0.6 copy-start.17
  67.7 1.6 copy-start.21
  69.3 15.4 %copy-start.4 = (f32[4096,128]{1,0:T(8,128)S(1)}, f32[4096,128]{1,0:T(8,128)}, u32[]{:S(2)}) copy-start(f32[4096,128]{1,0:T(8,128)} %copy-done.3) | copy-start | bytes 6291460
  69.3 15.4 %copy-start.11 = (f32[8,16,128]{2,1,0:T(8,128)S(1)}, f32[8,16,128]{2,1,0:T(8,128)}, u32[]{:S(2)}) copy-start(f32[8,16,128]{2,1,0:T(8,128)} %get-tuple-element.41.back) | copy-start | bytes 196612
  82.8 1.9 %copy-start = (f32[8192,128]{1,0:T(8,128)}, f32[8192,128]{1,0:T(8,128)S(1)}, u32[]{:S(2)}) copy-start(f32[8192,128]{1,0:T(8,128)S(1)} %shard_map.100.x0) | copy-start | bytes 12582916
where the time goes:
time: 180 us; the launch traced here: 179 us
  Pallas kernels  155 us (86%)
  local copies, waits for them, and re-layouts  20.2 us (11%)
  other arithmetic  2.23 us (1%)
    pallas_call x1, Pallas kernels, ring_sum(): pl.pallas_call(functools.partial(ring_kernel, n, count), out_shape=[jax.S...  91.9 us
    pallas_call x3, Pallas kernels, exchange(): pl.pallas_call(functools.partial(exchange_kernel, axis, n, spread), out_s...  24.3 us
    unnamed x48, local copies, waits for them, and re-layouts  19.7 us
    pallas_call x1, Pallas kernels, body(): call(functools.partial(gather_kernel, count), [SMEM, SMEM, VMEM, VMEM, VM...  14.1 us
    pallas_call x1, Pallas kernels, body(): call(scatter_excite_kernel, [SMEM] + [VMEM] * 2, [((types, slices), F32)]...  13.5 us
    pallas_call x1, Pallas kernels, body(): call(functools.partial(inside_kernel, count), [SMEM, SMEM] + [VMEM] * 4,...  5.29 us
    pallas_call x1, Pallas kernels, body(): call(functools.partial(forward_kernel, count, rank), [SMEM, SMEM, SMEM] +...  4.21 us

commit v1 on v0

v1 whole, which is shorter than its diff:
```python
import functools

import jax
import jax.numpy as jnp
from jax import lax
from jax.experimental import pallas as pl
from jax.experimental.pallas import tpu as pltpu
from jax.sharding import PartitionSpec as P

F32 = jnp.float32
BF16 = jnp.bfloat16
B = 128
SUB = 32
PARTS = B // SUB
HIGH = lax.Precision.HIGHEST
MESH = pl.DeviceIdType.MESH
VMEM = pl.BlockSpec(memory_space=pltpu.VMEM)
SMEM = pl.BlockSpec(memory_space=pltpu.SMEM)
ANY = pl.BlockSpec(memory_space=pl.ANY)
NT = (((1,), (1,)), ((), ()))


def iota(shape, axis):
    return lax.broadcasted_iota(jnp.int32, shape, axis)


def dot(a, b):
    return jnp.dot(a, b, preferred_element_type=F32)


def halves(a):
    high = a.astype(BF16).astype(F32)
    return high, a - high


def down(ref, count):
    row = iota((count, B), 0)
    out = jnp.zeros((count, B), F32)
    for k in range(count):
        out = jnp.where(row == k, ref[k], out)
    return out


def parted(a):
    part = lax.div(iota(a.shape, 1), SUB)
    return jnp.concatenate([jnp.where(part == c, a, 0.0) for c in range(PARTS)], 0)


def turned(row):
    return jnp.broadcast_to(row, (B, B)).T


def rows_at(b, size):
    return pl.ds(pl.multiple_of(b * size, size), size)


def front_kernel(
    n, lanes_n, rank,
    weights, decay, marks, gaps, src, exc, base,
    values, grad_base, minus, marks_out,
    factors, table, rows, smarks, own, gshard, u, te, ts, sym, inside, lanes, states, sums, dec, base_e,
    inverse, remain, ends, device, summaries, partial, total, back, behind, base_own, base_parts,
    load_sem, mark_sem, ag_send, ag_recv, f_send, f_recv, p_send, p_recv, b_send, b_recv, g_send, g_recv,
):
    count = decay.shape[0]
    width = count * PARTS
    half = n // 2
    shard_blocks = marks.shape[0]
    blocks = 2 * shard_blocks
    types = table.shape[0]
    groups = types // B
    ranks = src.shape[0] // 2
    edge = B // 2
    me = lax.axis_index("tm")
    mine = lax.axis_index("mark")
    r = lax.div(me, half)
    q = lax.rem(me, half)
    peers = [lax.rem(me + i, n) for i in range(1, n)]
    mates = [r * half + lax.rem(q + i, half) for i in range(1, half)]
    others = [lax.rem(mine + i, lanes_n) for i in range(1, lanes_n)]
    twin = q + (1 - r) * half

    if ranks < edge:
        for a in range(2):
            factors[a * edge + ranks : (a + 1) * edge, :] = jnp.zeros((edge - ranks, types), BF16)
    loads = []
    for a, ref in enumerate((src, exc)):
        copy = pltpu.make_async_copy(
            ref.at[pl.ds(pl.multiple_of(r * ranks, ranks), ranks), :],
            factors.at[a * edge : a * edge + ranks, :],
            load_sem.at[a],
        )
        copy.start()
        loads.append(copy)

    barrier = pltpu.get_barrier_semaphore()
    targets = [{"tm": p, "mark": mine} for p in peers]
    targets += [{"tm": t, "mark": o} for o in others for t in (me, twin)]
    for t in targets:
        pl.semaphore_signal(barrier, inc=1, device_id=t, device_id_type=MESH)
    pl.semaphore_wait(barrier, len(targets))

    slot = lax.rem(me, 2)
    own[...] = marks[...]

    def shard_copy(a, i, j, target):
        ref, dst = ((own, marks_out), (gaps, gshard))[a]
        return pltpu.make_async_remote_copy(
            src_ref=ref, dst_ref=dst.at[j], send_sem=ag_send.at[a, i], recv_sem=ag_recv.at[a, j],
            device_id={"tm": target}, device_id_type=MESH,
        )

    dests = [lax.div(me, 2) + i * half for i in range(2)]
    for i, p in enumerate(dests):

        @pl.when(p != me)
        def _():
            for a in range(2):
                shard_copy(a, i, slot, p).start()

        @pl.when(p == me)
        def _():
            marks_out[slot] = marks[...]
            gshard[slot] = gaps[...]

    for copy in loads:
        copy.wait()

    def build(c, acc):
        s = rows_at(c, B)
        t = factors[:, s].astype(F32).T
        table[s, :] = t
        return acc + jnp.sum(t.reshape(B // 8, 8, B), axis=0)

    acc = lax.fori_loop(0, groups, build, jnp.zeros((8, B), F32), unroll=2)
    xtot = jnp.sum(acc, axis=0, keepdims=True)

    for j in range(2):

        @pl.when(2 * q + j != me)
        def _():
            for a in range(2):
                shard_copy(a, 0, j, twin).wait_recv()

    move = pltpu.make_async_copy(marks_out, smarks, mark_sem.at[0])
    move.start()

    d8, w8 = down(decay, count), down(weights, count)
    gap_all = jnp.concatenate([gshard[0], gshard[1]], 0).astype(F32)
    li, lj = iota((B, B), 0), iota((B, B), 1)
    first = lax.div(lj, SUB) * SUB

    def pick(mask, a):
        return jnp.dot(a, mask.astype(F32), precision=HIGH, preferred_element_type=F32)

    uv = pick(li <= lj, gap_all)
    u[...] = uv
    te[...] = pick(li <= first + SUB - 1, gap_all)
    ts[...] = pick(li < first, gap_all)
    lengths = jnp.broadcast_to(uv[:, B - 1 :], (blocks, B))
    after_mask = (iota((blocks, blocks), 1) > iota((blocks, blocks), 0)).astype(F32)
    endv = jnp.dot(after_mask, lengths, precision=HIGH, preferred_element_type=F32)
    ends[...] = endv
    duration = endv[0:1, :] + lengths[0:1, :]
    move.wait()

    for j in range(2):

        def fetch(b, _):
            def some(g, _):
                for i in range(16):
                    m = smarks[j, b, g * 16 + i]
                    e = (j * shard_blocks + b) * B + g * 16 + i
                    rows[pl.ds(e, 1), :] = table[pl.ds(m, 1), :]
                return 0

            lax.fori_loop(0, B // 16, some, 0)
            return 0

        lax.fori_loop(0, shard_blocks, fetch, 0)

    part_row = lax.div(iota((1, B), 1), SUB)
    lane = iota((1, B), 1)

    def two(a, b):
        k = a.shape[0]
        high, low = halves(a)
        both = dot(jnp.concatenate([high, low], 0).astype(BF16), b)
        return both[:k] + both[k:]

    def emit(b, _):
        ur, er, sr = u[pl.ds(b, 1), :], te[pl.ds(b, 1), :], ts[pl.ds(b, 1), :]
        vals = rows[rows_at(b, B), :].astype(BF16)
        sums[rows_at(b, width), :] = two(parted(d8 * jnp.exp(-d8 * (er - ur))), vals)
        span = er - sr
        for c in range(PARTS):
            dec[pl.ds(pl.multiple_of(b * width + c * count, count), count), :] = jnp.exp(
                -d8 * span[:, c * SUB : c * SUB + 1]
            )
        return 0

    lax.fori_loop(0, blocks, emit, 0, unroll=4)

    def forward_state(start, keep):
        def step(b, state):
            for c in range(PARTS):
                s = pl.ds(pl.multiple_of(b * width + c * count, count), count)
                if keep:
                    states[s, :] = state
                state = state * dec[s, :] + sums[s, :]
            return state

        return lax.fori_loop(0, blocks, step, start, unroll=2)

    def share(source, dest, send, recv):
        copies = []
        for i, p in enumerate(mates):
            copies.append(
                pltpu.make_async_remote_copy(
                    src_ref=source, dst_ref=dest.at[q], send_sem=send.at[i], recv_sem=recv.at[i],
                    device_id={"tm": p}, device_id_type=MESH,
                )
            )
        for copy in copies:
            copy.start()
        dest[q] = source[...]
        return copies

    device[0:count, :] = forward_state(jnp.zeros((count, B), F32), False)
    device[count:, :] = jnp.broadcast_to(duration, (count, B))
    state_copies = share(device, summaries, f_send, f_recv)

    base_high, base_low = halves(base[...])
    base2 = jnp.concatenate([base_high, base_low], 0).T.astype(BF16)
    subi = iota((SUB, B), 0)
    subj = lax.rem(iota((SUB, B), 1), SUB)

    def mark_row(b):
        return marks_out[lax.div(b, shard_blocks), pl.ds(lax.rem(b, shard_blocks), 1), :]

    def within(b, _):
        ur, sr = u[pl.ds(b, 1), :], ts[pl.ds(b, 1), :]
        s = rows_at(b, B)
        col = turned(ur)
        colc = col[0:SUB]
        for c in range(1, PARTS):
            colc = jnp.where(part_row == c, col[c * SUB : (c + 1) * SUB], colc)
        apart = jnp.abs(colc - ur)
        g = jnp.zeros((SUB, B), F32)
        for k in range(count):
            g = g + (weights[k] * decay[k]) * jnp.exp(-decay[k] * apart)
        sym[rows_at(b, SUB), :] = g
        high, low = halves(jnp.where(subi > subj, g, 0.0))
        left = jnp.concatenate([parted(high), parted(low)], 0).astype(BF16)
        both = dot(left, rows[s, :].astype(BF16))
        inside[s, :] = both[:B] + both[B:]
        lh, ll = halves(parted(w8 * jnp.exp(-d8 * (ur - sr))))
        stack = jnp.concatenate([lh, lh, ll, jnp.zeros((B - 3 * width, B), F32)], 0)
        lanes[s, :] = stack.T.astype(BF16)
        m = mark_row(b)
        hi, lo = lax.div(m, B), lax.rem(m, B)
        onehot = (lax.rem(iota((2 * groups, B), 0), groups) == hi).astype(BF16)
        found = dot(base2, onehot)
        base_e[pl.ds(b, 1), :] = jnp.sum(jnp.where(li == lo, found, 0.0), axis=0, keepdims=True)
        return 0

    lax.fori_loop(0, blocks, within, 0, unroll=2)

    for copy in state_copies:
        copy.wait()
    start = jnp.zeros((count, B), F32)
    after = jnp.zeros((1, B), F32)
    t_end = jnp.zeros((1, B), F32)
    for p in range(half):
        span = summaries[p, count : count + 1, :]
        start = jnp.where(p < q, start * jnp.exp(-d8 * span) + summaries[p, 0:count, :], start)
        after = after + jnp.where(p > q, span, 0.0)
        t_end = t_end + span
    forward_state(start, True)

    ones = jnp.ones((8, B), BF16)
    fill = jnp.zeros((B - 3 * width, B), F32)

    def forward(b, _):
        s = rows_at(b, B)
        sh, sl = halves(states[rows_at(b, width), :])
        value = inside[s, :] + dot(lanes[s, :], jnp.concatenate([sh, sl, sh, fill], 0).astype(BF16))
        inside[s, :] = value
        product = jnp.where(lane < edge, value * pltpu.roll(rows[s, :], edge, 1), 0.0)
        high, low = halves(product)
        tot = lax.dot_general(ones, high.astype(BF16), NT, preferred_element_type=F32)
        tot = tot + lax.dot_general(ones, low.astype(BF16), NT, preferred_element_type=F32)
        partial[pl.ds(b, 1), :] = tot[0:1, :] * (1.0 / rank)
        return 0

    lax.fori_loop(0, blocks, forward, 0, unroll=2)

    spot = mine * 2 + r
    part_copies = []
    for i, t in enumerate([(twin, mine)] + [(t, o) for o in others for t in (me, twin)]):
        copy = pltpu.make_async_remote_copy(
            src_ref=partial, dst_ref=total.at[spot], send_sem=p_send.at[i], recv_sem=p_recv.at[i],
            device_id={"tm": t[0], "mark": t[1]}, device_id_type=MESH,
        )
        copy.start()
        part_copies.append(copy)
    total[spot] = partial[...]

    def rest(b, comp):
        left = w8 * (1.0 - jnp.exp(-d8 * (u[pl.ds(b, 1), :] * -1.0 + lengths_row(b) + ends[pl.ds(b, 1), :] + after)))
        rem = jnp.sum(left, axis=0, keepdims=True)
        remain[pl.ds(b, 1), :] = rem
        return comp + two(jnp.broadcast_to(rem, (8, B)), rows[rows_at(b, B), :].astype(BF16))

    def lengths_row(b):
        return u[pl.ds(b, 1), B - 1 :]

    comp = lax.fori_loop(0, blocks, rest, jnp.zeros((8, B), F32), unroll=4)

    for copy in part_copies:
        copy.wait()
    intensity = base_e[...]
    for j in range(2 * lanes_n):
        intensity = intensity + total[j]
    inverse[...] = 1.0 / intensity

    def reverse(b, _):
        e8 = d8 * jnp.exp(-d8 * (u[pl.ds(b, 1), :] - ts[pl.ds(b, 1), :])) * inverse[pl.ds(b, 1), :]
        sums[rows_at(b, width), :] = two(parted(e8), rows[rows_at(b, B), :].astype(BF16))
        return 0

    lax.fori_loop(0, blocks, reverse, 0, unroll=4)

    def reverse_state(start, keep):
        def step(i, state):
            b = blocks - 1 - i
            for c in reversed(range(PARTS)):
                s = pl.ds(pl.multiple_of(b * width + c * count, count), count)
                if keep:
                    states[s, :] = state
                state = state * dec[s, :] + sums[s, :]
            return state

        return lax.fori_loop(0, blocks, step, start, unroll=2)

    behind[0:count, :] = reverse_state(jnp.zeros((count, B), F32), False)
    behind[count:, :] = comp
    back_copies = share(behind, back, b_send, b_recv)

    def spread(i, both):
        b = r * shard_blocks + i
        m = mark_row(b)
        hi, lo = lax.div(m, B), lax.rem(m, B)
        ih, il = halves(inverse[pl.ds(b, 1), :])
        wide = jnp.concatenate([jnp.broadcast_to(ih, (groups, B)), jnp.broadcast_to(il, (groups, B))], 0)
        left = jnp.where(lax.rem(iota((2 * groups, B), 0), groups) == hi, wide, 0.0).astype(BF16)
        right = (li == lo).astype(BF16)
        return both + lax.dot_general(left, right, NT, preferred_element_type=F32)

    both = lax.fori_loop(0, shard_blocks, spread, jnp.zeros((2 * groups, B), F32), unroll=2)
    base_own[...] = (both[:groups] + both[groups:]).reshape(base_own.shape)
    base_copies = []
    for i, p in enumerate(peers):
        copy = pltpu.make_async_remote_copy(
            src_ref=base_own.at[p], dst_ref=base_parts.at[me], send_sem=g_send.at[i], recv_sem=g_recv.at[i],
            device_id={"tm": p}, device_id_type=MESH,
        )
        copy.start()
        base_copies.append(copy)
    base_parts[me] = base_own[me]

    for copy in back_copies:
        copy.wait()
    pending = jnp.zeros((count, B), F32)
    comp_all = jnp.zeros((8, B), F32)
    for p in reversed(range(half)):
        span = summaries[p, count : count + 1, :]
        pending = jnp.where(p > q, pending * jnp.exp(-d8 * span) + back[p, 0:count, :], pending)
        comp_all = comp_all + back[p, count:, :]
    reverse_state(pending, True)
    events_all = blocks * B * half
    minus[...] = jnp.where(lane < edge, comp_all * (1.0 / events_all), 0.0)

    row8 = iota((8, B), 0)

    def thirds(a, places):
        high, rest = halves(a)
        mid, low = halves(rest)
        out = jnp.zeros((8, B), F32)
        for term, where in zip((high, mid, low), places):
            for k in where:
                out = jnp.where(row8 == k, term, out)
        return out

    xstack = thirds(xtot * (-1.0 / types), ((0, 2, 5), (1, 4), (3,)))
    fill24 = jnp.zeros((B - 3 * width - 8, B), F32)

    def feedback(b, _):
        s = rows_at(b, B)
        ur, er, ir = u[pl.ds(b, 1), :], te[pl.ds(b, 1), :], inverse[pl.ds(b, 1), :]
        high, low = halves(jnp.where(subi < subj, sym[rows_at(b, SUB), :] * ir, 0.0))
        left = jnp.concatenate([parted(high), parted(low)], 0).astype(BF16)
        both = dot(left, rows[s, :].astype(BF16))
        lh, ll = halves(parted(w8 * jnp.exp(-d8 * (er - ur))))
        rstack = thirds(remain[pl.ds(b, 1), :], ((0, 1, 3), (2, 4), (5,)))
        turn = jnp.concatenate([lh, lh, ll, rstack, fill24], 0).T.astype(BF16)
        sh, sl = halves(states[rows_at(b, width), :])
        value = both[:B] + both[B:] + dot(
            turn, jnp.concatenate([sh, sl, sh, xstack, fill24], 0).astype(BF16)
        )
        values[s, :] = jnp.where(lane < edge, inside[s, :] * turned(ir), value)
        return 0

    lax.fori_loop(0, blocks, feedback, 0, unroll=2)

    for copy in base_copies:
        copy.wait()
    base_all = base_parts[0]
    for p in range(1, n):
        base_all = base_all + base_parts[p]
    grad_base[...] = base_all * (types / events_all) - t_end * (1.0 / events_all)
    for i, p in enumerate(dests):

        @pl.when(p != me)
        def _():
            for a in range(2):
                shard_copy(a, i, slot, p).wait_send()


def scatter_kernel(marks, values, out, *tables):
    count = len(tables) + 1
    every = (out,) + tables
    types = out.shape[0]

    def zero(i, _):
        for t in every:
            t[pl.ds(pl.multiple_of(i * 32, 32), 32), :] = jnp.zeros((32, B), F32)
        return 0

    lax.fori_loop(0, types // 32, zero, 0)
    shards, blocks, _ = marks.shape
    group = 2 * count
    for j in range(shards):

        def block(b, _):
            def some(g, _):
                for i in range(group):
                    t = every[i % count]
                    m = marks[j, b, g * group + i]
                    e = (j * blocks + b) * B + g * group + i
                    t[pl.ds(m, 1), :] = t[pl.ds(m, 1), :] + values[pl.ds(e, 1), :]
                return 0

            lax.fori_loop(0, B // group, some, 0)
            return 0

        lax.fori_loop(0, blocks, block, 0)

    def add(i, _):
        s = pl.ds(pl.multiple_of(i * 32, 32), 32)
        acc = out[s, :]
        for t in tables:
            acc = acc + t[s, :]
        out[s, :] = acc
        return 0

    lax.fori_loop(0, types // 32, add, 0)


def ring_kernel(n, factor, minus, dense, grad_excite, grad_source, slots, pieces, twin_in, send, recv, t_send, t_recv):
    half = n // 2
    per = dense.shape[0] // n
    rows = per // 2
    edge = B // 2
    ranks = grad_excite.shape[0] // 2
    me = lax.axis_index("tm")
    r = lax.div(me, half)
    q = lax.rem(me, half)
    odd = lax.rem(q, 2)
    at = lax.div(q, 2) + odd * (lax.div(2 * half - 1 - q, 2) - lax.div(q, 2))
    twin = q + (1 - r) * half

    def member(place):
        c = lax.rem(place + 2 * half, half)
        return 2 * c + lax.div(c, half // 2) * (2 * half - 1 - 4 * c)

    towards = [member(at + 1) + r * half, member(at - 1) + r * half]
    barrier = pltpu.get_barrier_semaphore()
    for p in towards + [twin]:
        pl.semaphore_signal(barrier, inc=1, device_id={"tm": p}, device_id_type=MESH)
    pl.semaphore_wait(barrier, 3)

    def span(j, step):
        way, kind = j % 2, j // 2
        place = at + 1 + step if way else at - 1 - step
        where = (1 - r) if kind == 0 else r
        block = member(place) + where * half
        return pl.ds(pl.multiple_of(block * per + way * rows, 8), rows)

    def copy(j, step, source):
        return pltpu.make_async_remote_copy(
            src_ref=source, dst_ref=slots.at[j, step], send_sem=send.at[j, step], recv_sem=recv.at[j, step],
            device_id={"tm": towards[j % 2]}, device_id_type=MESH,
        )

    chains = range(4)
    for j in chains:
        copy(j, 0, dense.at[span(j, 0), :]).start()

    def step(s, _):
        for j in chains:
            held = slots.at[j, s - 1]
            copy(j, s - 1, held).wait_recv()
            held[...] += dense[span(j, s), :]
            copy(j, s, held).start()
        return 0

    lax.fori_loop(1, half - 1, step, 0)

    def twin_copy(j):
        return pltpu.make_async_remote_copy(
            src_ref=pieces.at[j], dst_ref=twin_in.at[j], send_sem=t_send.at[j], recv_sem=t_recv.at[j],
            device_id={"tm": twin}, device_id_type=MESH,
        )

    for j in chains:
        copy(j, half - 2, slots.at[j, half - 2]).wait_recv()
        pieces[j] = (slots[j, half - 2] + dense[span(j, half - 1), :]) * factor - minus[0:1, :]
        if j < 2:
            twin_copy(j).start()
    low = r == 0
    for j in range(2):
        twin_copy(j).wait_recv()
        for i in range(rows // B):
            s = slice(i * B, (i + 1) * B)
            mine, their = pieces[2 + j, s, :].T, twin_in[j, s, :].T
            first = jnp.where(low, mine, their)
            second = jnp.where(low, their, mine)
            t = slice(j * rows + i * B, j * rows + (i + 1) * B)
            grad_excite[:ranks, t] = first[:ranks]
            grad_excite[ranks:, t] = second[:ranks]
            grad_source[:ranks, t] = first[edge : edge + ranks]
            grad_source[ranks:, t] = second[edge : edge + ranks]

    def sent(s, _):
        for j in chains:
            copy(j, s, slots.at[j, s]).wait_send()
        return 0

    lax.fori_loop(0, half - 1, sent, 0)
    for j in range(2):
        twin_copy(j).wait_send()


def body(marks, gaps, excite, source, base_rate, weights, decay):
    shard = marks.shape[0]
    slices, types = excite.shape
    n = lax.axis_size("tm")
    lanes_n = lax.axis_size("mark")
    half = n // 2
    rank = slices * lanes_n
    count = decay.shape[0]
    shard_blocks = shard // B
    blocks = 2 * shard_blocks
    events = 2 * shard
    groups = types // B
    width = count * PARTS
    dma = pltpu.SemaphoreType.DMA
    plane = pltpu.VMEM((blocks, B), F32)
    tall = pltpu.VMEM((events, B), F32)
    small = pltpu.VMEM((blocks * width, B), F32)
    packet = pltpu.VMEM((count + 8, B), F32)
    packets = pltpu.VMEM((half, count + 8, B), F32)
    types_own = types // n

    values, grad_base, minus, marks_all = pl.pallas_call(
        functools.partial(front_kernel, n, lanes_n, rank),
        out_shape=[
            jax.ShapeDtypeStruct((events, B), F32),
            jax.ShapeDtypeStruct((groups // n, B), F32),
            jax.ShapeDtypeStruct((8, B), F32),
            jax.ShapeDtypeStruct((2, shard_blocks, B), jnp.int32),
        ],
        in_specs=[SMEM, SMEM, VMEM, VMEM, ANY, ANY, VMEM],
        out_specs=[VMEM] * 4,
        scratch_shapes=[
            pltpu.VMEM((B, types), BF16),
            pltpu.VMEM((types, B), F32),
            tall,
            pltpu.SMEM((2, shard_blocks, B), jnp.int32),
            pltpu.VMEM((shard_blocks, B), jnp.int32),
            pltpu.VMEM((2, shard_blocks, B), jnp.int32),
            plane, plane, plane,
            pltpu.VMEM((blocks * SUB, B), F32),
            tall,
            pltpu.VMEM((events, B), BF16),
            small, small, small,
            plane, plane, plane, plane,
            packet, packets,
            plane, pltpu.VMEM((2 * lanes_n, blocks, B), F32),
            packets, packet,
            pltpu.VMEM((n, groups // n, B), F32),
            pltpu.VMEM((n, groups // n, B), F32),
            dma((2,)), dma((1,)),
            dma((2, 2)), dma((2, 2)),
            dma((half - 1,)), dma((half - 1,)),
            dma((2 * lanes_n - 1,)), dma((2 * lanes_n - 1,)),
            dma((half - 1,)), dma((half - 1,)),
            dma((n - 1,)), dma((n - 1,)),
        ],
        compiler_params=pltpu.CompilerParams(
            collective_id=0, has_side_effects=True, vmem_limit_bytes=48 * 2**20
        ),
    )(weights, decay, marks.reshape(shard_blocks, B), gaps.reshape(shard_blocks, B), source, excite,
      base_rate.reshape(groups, B))

    dense = pl.pallas_call(
        scatter_kernel,
        out_shape=jax.ShapeDtypeStruct((types, B), F32),
        in_specs=[SMEM, VMEM],
        out_specs=VMEM,
        scratch_shapes=[pltpu.VMEM((types, B), F32)] * 3,
        compiler_params=pltpu.CompilerParams(vmem_limit_bytes=40 * 2**20),
    )(marks_all, values)

    grad_excite, grad_source = pl.pallas_call(
        functools.partial(ring_kernel, n, types / (events * half)),
        out_shape=[jax.ShapeDtypeStruct((slices, types_own), F32)] * 2,
        in_specs=[VMEM] * 2,
        out_specs=[VMEM] * 2,
        scratch_shapes=[
            pltpu.VMEM((4, half - 1, types_own // 2, B), F32),
            pltpu.VMEM((4, types_own // 2, B), F32),
            pltpu.VMEM((2, types_own // 2, B), F32),
            dma((4, half - 1)), dma((4, half - 1)), dma((2,)), dma((2,)),
        ],
        compiler_params=pltpu.CompilerParams(
            collective_id=1, has_side_effects=True, vmem_limit_bytes=40 * 2**20
        ),
    )(minus, dense)
    return grad_excite, grad_source, grad_base.reshape(types_own)


def solution(mesh):
    return jax.shard_map(
        body,
        mesh=mesh,
        in_specs=(P("tm"), P("tm"), P("mark", None), P("mark", None), P(), P(), P()),
        out_specs=(P("mark", "tm"), P("mark", "tm"), P("tm")),
        check_vma=False,
    )
```

time: 180 us -> 181 us (level)
  Pallas kernels: 155 us -> 169 us
  local copies, waits for them, and re-layouts: 20.2 us -> 11 us
  other arithmetic: 2.23 us -> 0 us
    pallas_call x9 -> x3, Pallas kernels: 155 us -> 169 us  [the longest x1 83.1 us: body(): pl.pallas_call(functools.partial(front_kernel, n, lanes_n, rank), out_sha...]
    unnamed x48 -> x19, local copies, waits for them, and re-layouts: 19.7 us -> 11 us
where the time goes in v1:
time: 181 us
  Pallas kernels  169 us (93%)
  local copies, waits for them, and re-layouts  11 us (6%)
    pallas_call x1, Pallas kernels, body(): pl.pallas_call(functools.partial(front_kernel, n, lanes_n, rank), out_sha...  83.1 us
    pallas_call x1, Pallas kernels, body(): pl.pallas_call(functools.partial(ring_kernel, n, types / (events * half))...  55.7 us
    pallas_call x1, Pallas kernels, body(): pl.pallas_call(scatter_kernel, out_shape=jax.ShapeDtypeStruct((types, B),...  30.3 us
    unnamed x19, local copies, waits for them, and re-layouts  11 us

profile of v1, /device:TPU:0, one launch (start us, length us, event | category | flops | bytes accessed | tf_op | source)
XLA Modules:
  0.0 180.8 jit_solution(5384908257100091208)
XLA Ops:
  0.6 0.0 copy-start.1
  0.6 1.6 copy-done.1
  2.2 0.0 copy-start.2
  2.2 1.6 copy-done.2
  3.8 0.0 copy-start.3
  3.8 0.8 copy-done.3
  4.6 0.0 copy-start.4
  4.6 0.7 copy-done.4
  5.3 0.0 copy-start.5
  5.3 0.7 copy-done.5
  6.0 0.0 copy-start.6
  6.0 0.7 copy-done.6
  6.7 0.0 copy-start.7
  6.7 0.7 copy-done.7
  7.3 83.1 %shard_map.94 = (f32[8192,128]{1,0:T(8,128)}, f32[8,128]{1,0:T(8,128)S(1)}, f32[8,128]{1,0:T(8,128)S(1)}, s32[2,32,128]{2,1,0:T(8,128)S(1)}) custom-call(f32[8]{0:T(128)S(1)} %copy-done.6, f32[8]{0:T(128)S(1)} %copy-done.7, s32[32,128]{1,0:T(8,128)S(1)} %bitcast.5, s32[32,128]{1,0:T(8,128)S(1)} %bitcast.6, bf16[128,8192]{1,0:T(8,128)(2,1)S(1)} %copy-done.1, ...), custom_call_target="tpu_custom_call" | custom-call | tf_op jit(solution)/shard_map/pallas_call | solution.py:576
  90.4 0.0 copy-start
  90.5 2.2 %copy-done = f32[8192,128]{1,0:T(8,128)S(1)} copy-done((f32[8192,128]{1,0:T(8,128)S(1)}, f32[8192,128]{1,0:T(8,128)}, u32[]{:S(2)}) %copy-start) | copy-done | bytes 4194328
  92.6 30.3 %shard_map.95.dense = f32[8192,128]{1,0:T(8,128)S(1)} custom-call(s32[2,32,128]{2,1,0:T(8,128)S(1)} %get-tuple-element.10.marks, f32[8192,128]{1,0:T(8,128)S(1)} %copy-done), custom_call_target="tpu_custom_call" | custom-call | tf_op jit(solution)/shard_map/pallas_call | solution.py:617
  122.9 55.7 %shard_map.96 = (f32[128,1024]{1,0:T(8,128)S(1)}, f32[128,1024]{1,0:T(8,128)S(1)}) custom-call(f32[8,128]{1,0:T(8,128)S(1)} %get-tuple-element.9.minus, f32[8192,128]{1,0:T(8,128)S(1)} %shard_map.95.dense), custom_call_target="tpu_custom_call" | custom-call | tf_op jit(solution)/shard_map/pallas_call | solution.py:626
  178.6 0.8 copy.13
  179.4 0.8 copy.14
  180.2 0.6 copy.15
Async XLA Ops:
  0.6 1.6 copy-start.1
  2.2 1.6 copy-start.2
  3.8 0.8 copy-start.3
  4.6 0.7 copy-start.4
  5.3 0.7 copy-start.5
  6.0 0.7 copy-start.6
  6.7 0.7 copy-start.7
  90.4 2.2 %copy-start = (f32[8192,128]{1,0:T(8,128)S(1)}, f32[8192,128]{1,0:T(8,128)}, u32[]{:S(2)}) copy-start(f32[8192,128]{1,0:T(8,128)} %get-tuple-element.11.values) | copy-start | bytes 12582916

commit v2 on v1

--- a/solution.py
+++ b/solution.py
@@ -11,12 +11,13 @@
 BF16 = jnp.bfloat16
 B = 128
 SUB = 32
+UNROLL = 16
 PARTS = B // SUB
 HIGH = lax.Precision.HIGHEST
 MESH = pl.DeviceIdType.MESH
 VMEM = pl.BlockSpec(memory_space=pltpu.VMEM)
 SMEM = pl.BlockSpec(memory_space=pltpu.SMEM)
-ANY = pl.BlockSpec(memory_space=pl.ANY)
+HBM = pl.BlockSpec(memory_space=pltpu.HBM)
 NT = (((1,), (1,)), ((), ()))
 
 
@@ -50,6 +51,18 @@
     return jnp.broadcast_to(row, (B, B)).T
 
 
+def batched(count, size, one):
+    def body(g, _):
+        stores = []
+        for i in range(size):
+            stores += one(g * size + i)
+        for ref, where, value in stores:
+            ref[where] = value
+        return 0
+
+    lax.fori_loop(0, count // size, body, 0)
+
+
 def rows_at(b, size):
     return pl.ds(pl.multiple_of(b * size, size), size)
 
@@ -58,7 +71,7 @@
     n, lanes_n, rank,
     weights, decay, marks, gaps, src, exc, base,
     values, grad_base, minus, marks_out,
-    factors, table, rows, smarks, own, gshard, u, te, ts, sym, inside, lanes, states, sums, dec, base_e,
+    factors, table, rows, smarks, own, gshard, u, te, ts, sym, inside, excitation, lanes, states, sums, dec, base_e,
     inverse, remain, ends, device, summaries, partial, total, back, behind, base_own, base_parts,
     load_sem, mark_sem, ag_send, ag_recv, f_send, f_recv, p_send, p_recv, b_send, b_recv, g_send, g_recv,
 ):
@@ -132,7 +145,7 @@
         table[s, :] = t
         return acc + jnp.sum(t.reshape(B // 8, 8, B), axis=0)
 
-    acc = lax.fori_loop(0, groups, build, jnp.zeros((8, B), F32), unroll=2)
+    acc = lax.fori_loop(0, groups, build, jnp.zeros((8, B), F32), unroll=8)
     xtot = jnp.sum(acc, axis=0, keepdims=True)
 
     for j in range(2):
@@ -166,15 +179,11 @@
 
     for j in range(2):
 
-        def fetch(b, _):
-            def some(g, _):
-                for i in range(16):
-                    m = smarks[j, b, g * 16 + i]
-                    e = (j * shard_blocks + b) * B + g * 16 + i
-                    rows[pl.ds(e, 1), :] = table[pl.ds(m, 1), :]
-                return 0
-
-            lax.fori_loop(0, B // 16, some, 0)
+        def fetch(g, _):
+            for i in range(B):
+                m = smarks[j, g, i]
+                e = (j * shard_blocks + g) * B + i
+                rows[pl.ds(e, 1), :] = table[pl.ds(m, 1), :]
             return 0
 
         lax.fori_loop(0, shard_blocks, fetch, 0)
@@ -188,18 +197,18 @@
         both = dot(jnp.concatenate([high, low], 0).astype(BF16), b)
         return both[:k] + both[k:]
 
-    def emit(b, _):
+    def emit(b):
         ur, er, sr = u[pl.ds(b, 1), :], te[pl.ds(b, 1), :], ts[pl.ds(b, 1), :]
         vals = rows[rows_at(b, B), :].astype(BF16)
-        sums[rows_at(b, width), :] = two(parted(d8 * jnp.exp(-d8 * (er - ur))), vals)
         span = er - sr
-        for c in range(PARTS):
-            dec[pl.ds(pl.multiple_of(b * width + c * count, count), count), :] = jnp.exp(
-                -d8 * span[:, c * SUB : c * SUB + 1]
-            )
-        return 0
-
-    lax.fori_loop(0, blocks, emit, 0, unroll=4)
+        decays = [jnp.exp(-d8 * span[:, c * SUB : c * SUB + 1]) for c in range(PARTS)]
+        spot = (rows_at(b, width), slice(None))
+        return [
+            (sums, spot, two(parted(d8 * jnp.exp(-d8 * (er - ur))), vals)),
+            (dec, spot, jnp.concatenate([jnp.broadcast_to(t, (count, B)) for t in decays], 0)),
+        ]
+
+    batched(blocks, UNROLL, emit)
 
     def forward_state(start, keep):
         def step(b, state):
@@ -238,7 +247,7 @@
     def mark_row(b):
         return marks_out[lax.div(b, shard_blocks), pl.ds(lax.rem(b, shard_blocks), 1), :]
 
-    def within(b, _):
+    def within(b):
         ur, sr = u[pl.ds(b, 1), :], ts[pl.ds(b, 1), :]
         s = rows_at(b, B)
         col = turned(ur)
@@ -249,22 +258,23 @@
         g = jnp.zeros((SUB, B), F32)
         for k in range(count):
             g = g + (weights[k] * decay[k]) * jnp.exp(-decay[k] * apart)
-        sym[rows_at(b, SUB), :] = g
         high, low = halves(jnp.where(subi > subj, g, 0.0))
         left = jnp.concatenate([parted(high), parted(low)], 0).astype(BF16)
         both = dot(left, rows[s, :].astype(BF16))
-        inside[s, :] = both[:B] + both[B:]
         lh, ll = halves(parted(w8 * jnp.exp(-d8 * (ur - sr))))
         stack = jnp.concatenate([lh, lh, ll, jnp.zeros((B - 3 * width, B), F32)], 0)
-        lanes[s, :] = stack.T.astype(BF16)
         m = mark_row(b)
         hi, lo = lax.div(m, B), lax.rem(m, B)
         onehot = (lax.rem(iota((2 * groups, B), 0), groups) == hi).astype(BF16)
         found = dot(base2, onehot)
-        base_e[pl.ds(b, 1), :] = jnp.sum(jnp.where(li == lo, found, 0.0), axis=0, keepdims=True)
-        return 0
-
-    lax.fori_loop(0, blocks, within, 0, unroll=2)
+        return [
+            (sym, (rows_at(b, SUB), slice(None)), g),
+            (inside, (s, slice(None)), both[:B] + both[B:]),
+            (lanes, (s, slice(None)), stack.T.astype(BF16)),
+            (base_e, (pl.ds(b, 1), slice(None)), jnp.sum(jnp.where(li == lo, found, 0.0), axis=0, keepdims=True)),
+        ]
+
+    batched(blocks, UNROLL, within)
 
     for copy in state_copies:
         copy.wait()
@@ -281,19 +291,20 @@
     ones = jnp.ones((8, B), BF16)
     fill = jnp.zeros((B - 3 * width, B), F32)
 
-    def forward(b, _):
+    def forward(b):
         s = rows_at(b, B)
         sh, sl = halves(states[rows_at(b, width), :])
         value = inside[s, :] + dot(lanes[s, :], jnp.concatenate([sh, sl, sh, fill], 0).astype(BF16))
-        inside[s, :] = value
         product = jnp.where(lane < edge, value * pltpu.roll(rows[s, :], edge, 1), 0.0)
         high, low = halves(product)
         tot = lax.dot_general(ones, high.astype(BF16), NT, preferred_element_type=F32)
         tot = tot + lax.dot_general(ones, low.astype(BF16), NT, preferred_element_type=F32)
-        partial[pl.ds(b, 1), :] = tot[0:1, :] * (1.0 / rank)
-        return 0
-
-    lax.fori_loop(0, blocks, forward, 0, unroll=2)
+        return [
+            (excitation, (s, slice(None)), value),
+            (partial, (pl.ds(b, 1), slice(None)), tot[0:1, :] * (1.0 / rank)),
+        ]
+
+    batched(blocks, UNROLL, forward)
 
     spot = mine * 2 + r
     part_copies = []
@@ -324,12 +335,11 @@
         intensity = intensity + total[j]
     inverse[...] = 1.0 / intensity
 
-    def reverse(b, _):
+    def reverse(b):
         e8 = d8 * jnp.exp(-d8 * (u[pl.ds(b, 1), :] - ts[pl.ds(b, 1), :])) * inverse[pl.ds(b, 1), :]
-        sums[rows_at(b, width), :] = two(parted(e8), rows[rows_at(b, B), :].astype(BF16))
-        return 0
-
-    lax.fori_loop(0, blocks, reverse, 0, unroll=4)
+        return [(sums, (rows_at(b, width), slice(None)), two(parted(e8), rows[rows_at(b, B), :].astype(BF16)))]
+
+    batched(blocks, UNROLL, reverse)
 
     def reverse_state(start, keep):
         def step(i, state):
@@ -395,7 +405,7 @@
     xstack = thirds(xtot * (-1.0 / types), ((0, 2, 5), (1, 4), (3,)))
     fill24 = jnp.zeros((B - 3 * width - 8, B), F32)
 
-    def feedback(b, _):
+    def feedback(b):
         s = rows_at(b, B)
         ur, er, ir = u[pl.ds(b, 1), :], te[pl.ds(b, 1), :], inverse[pl.ds(b, 1), :]
         high, low = halves(jnp.where(subi < subj, sym[rows_at(b, SUB), :] * ir, 0.0))
@@ -408,10 +418,9 @@
         value = both[:B] + both[B:] + dot(
             turn, jnp.concatenate([sh, sl, sh, xstack, fill24], 0).astype(BF16)
         )
-        values[s, :] = jnp.where(lane < edge, inside[s, :] * turned(ir), value)
-        return 0
-
-    lax.fori_loop(0, blocks, feedback, 0, unroll=2)
+        return [(values, (s, slice(None)), jnp.where(lane < edge, excitation[s, :] * turned(ir), value))]
+
+    batched(blocks, UNROLL, feedback)
 
     for copy in base_copies:
         copy.wait()
@@ -439,19 +448,14 @@
 
     lax.fori_loop(0, types // 32, zero, 0)
     shards, blocks, _ = marks.shape
-    group = 2 * count
     for j in range(shards):
 
         def block(b, _):
-            def some(g, _):
-                for i in range(group):
-                    t = every[i % count]
-                    m = marks[j, b, g * group + i]
-                    e = (j * blocks + b) * B + g * group + i
-                    t[pl.ds(m, 1), :] = t[pl.ds(m, 1), :] + values[pl.ds(e, 1), :]
-                return 0
-
-            lax.fori_loop(0, B // group, some, 0)
+            for i in range(B):
+                t = every[i % count]
+                m = marks[j, b, i]
+                e = (j * blocks + b) * B + i
+                t[pl.ds(m, 1), :] = t[pl.ds(m, 1), :] + values[pl.ds(e, 1), :]
             return 0
 
         lax.fori_loop(0, blocks, block, 0)
@@ -581,7 +585,7 @@
             jax.ShapeDtypeStruct((8, B), F32),
             jax.ShapeDtypeStruct((2, shard_blocks, B), jnp.int32),
         ],
-        in_specs=[SMEM, SMEM, VMEM, VMEM, ANY, ANY, VMEM],
+        in_specs=[SMEM, SMEM, VMEM, VMEM, HBM, HBM, VMEM],
         out_specs=[VMEM] * 4,
         scratch_shapes=[
             pltpu.VMEM((B, types), BF16),
@@ -592,7 +596,7 @@
             pltpu.VMEM((2, shard_blocks, B), jnp.int32),
             plane, plane, plane,
             pltpu.VMEM((blocks * SUB, B), F32),
-            tall,
+            tall, tall,
             pltpu.VMEM((events, B), BF16),
             small, small, small,
             plane, plane, plane, plane,
@@ -619,7 +623,7 @@
         out_shape=jax.ShapeDtypeStruct((types, B), F32),
         in_specs=[SMEM, VMEM],
         out_specs=VMEM,
-        scratch_shapes=[pltpu.VMEM((types, B), F32)] * 3,
+        scratch_shapes=[pltpu.VMEM((types, B), F32)] * 7,
         compiler_params=pltpu.CompilerParams(vmem_limit_bytes=40 * 2**20),
     )(marks_all, values)
 

time: 181 us -> 129 us (0.71)
  Pallas kernels: 169 us -> 117 us
    pallas_call x1, Pallas kernels: 83.1 us -> 49.5 us  [body(): pl.pallas_call(functools.partial(front_kernel, n, lanes_n, rank), out_sha...]
    pallas_call x1, Pallas kernels: 30.3 us -> 13.4 us  [body(): pl.pallas_call(scatter_kernel, out_shape=jax.ShapeDtypeStruct((types, B),...]
where the time goes in v2:
time: 129 us
  Pallas kernels  117 us (91%)
  local copies, waits for them, and re-layouts  11 us (9%)
    pallas_call x1, Pallas kernels, body(): pl.pallas_call(functools.partial(ring_kernel, n, types / (events * half))...  54 us
    pallas_call x1, Pallas kernels, body(): pl.pallas_call(functools.partial(front_kernel, n, lanes_n, rank), out_sha...  49.5 us
    pallas_call x1, Pallas kernels, body(): pl.pallas_call(scatter_kernel, out_shape=jax.ShapeDtypeStruct((types, B),...  13.4 us
    unnamed x19, local copies, waits for them, and re-layouts  11 us

profile of v2, /device:TPU:0, one launch (start us, length us, event | category | flops | bytes accessed | tf_op | source)
XLA Modules:
  0.0 128.6 jit_solution(5564280945419509325)
XLA Ops:
  0.6 0.0 copy-start.1
  0.6 1.6 %copy-done.1 = bf16[128,8192]{1,0:T(8,128)(2,1)S(1)} copy-done((bf16[128,8192]{1,0:T(8,128)(2,1)S(1)}, bf16[128,8192]{1,0:T(8,128)(2,1)}, u32[]{:S(2)}) %copy-start.1) | copy-done | bytes 2097176
  2.2 0.0 copy-start.2
  2.2 1.6 %copy-done.2 = bf16[128,8192]{1,0:T(8,128)(2,1)S(1)} copy-done((bf16[128,8192]{1,0:T(8,128)(2,1)S(1)}, bf16[128,8192]{1,0:T(8,128)(2,1)}, u32[]{:S(2)}) %copy-start.2) | copy-done | bytes 2097176
  3.8 0.0 copy-start.3
  3.8 0.8 copy-done.3
  4.6 0.0 copy-start.4
  4.6 0.7 copy-done.4
  5.3 0.0 copy-start.5
  5.3 0.7 copy-done.5
  6.0 0.0 copy-start.6
  6.0 0.7 copy-done.6
  6.7 0.0 copy-start.7
  6.7 0.7 copy-done.7
  7.3 49.5 %shard_map.94 = (f32[8192,128]{1,0:T(8,128)}, f32[8,128]{1,0:T(8,128)S(1)}, f32[8,128]{1,0:T(8,128)S(1)}, s32[2,32,128]{2,1,0:T(8,128)S(1)}) custom-call(f32[8]{0:T(128)S(1)} %copy-done.6, f32[8]{0:T(128)S(1)} %copy-done.7, s32[32,128]{1,0:T(8,128)S(1)} %bitcast.5, s32[32,128]{1,0:T(8,128)S(1)} %bitcast.6, bf16[128,8192]{1,0:T(8,128)(2,1)S(1)} %copy-done.1, ...), custom_call_target="tpu_custom_call" | custom-call | tf_op jit(solution)/shard_map/pallas_call | solution.py:580
  56.8 0.0 copy-start
  56.8 2.2 %copy-done = f32[8192,128]{1,0:T(8,128)S(1)} copy-done((f32[8192,128]{1,0:T(8,128)S(1)}, f32[8192,128]{1,0:T(8,128)}, u32[]{:S(2)}) %copy-start) | copy-done | bytes 4194328
  59.0 13.4 %shard_map.95.dense = f32[8192,128]{1,0:T(8,128)S(1)} custom-call(s32[2,32,128]{2,1,0:T(8,128)S(1)} %get-tuple-element.10.marks, f32[8192,128]{1,0:T(8,128)S(1)} %copy-done), custom_call_target="tpu_custom_call" | custom-call | tf_op jit(solution)/shard_map/pallas_call | solution.py:621
  72.4 54.0 %shard_map.96 = (f32[128,1024]{1,0:T(8,128)S(1)}, f32[128,1024]{1,0:T(8,128)S(1)}) custom-call(f32[8,128]{1,0:T(8,128)S(1)} %get-tuple-element.9.minus, f32[8192,128]{1,0:T(8,128)S(1)} %shard_map.95.dense), custom_call_target="tpu_custom_call" | custom-call | tf_op jit(solution)/shard_map/pallas_call | solution.py:630
  126.4 0.8 copy.13
  127.2 0.8 copy.14
  128.0 0.6 copy.15
Async XLA Ops:
  0.6 1.6 %copy-start.1 = (bf16[128,8192]{1,0:T(8,128)(2,1)S(1)}, bf16[128,8192]{1,0:T(8,128)(2,1)}, u32[]{:S(2)}) copy-start(bf16[128,8192]{1,0:T(8,128)(2,1)} %src.1) | copy-start | bytes 6291460
  2.2 1.6 %copy-start.2 = (bf16[128,8192]{1,0:T(8,128)(2,1)S(1)}, bf16[128,8192]{1,0:T(8,128)(2,1)}, u32[]{:S(2)}) copy-start(bf16[128,8192]{1,0:T(8,128)(2,1)} %exc.1) | copy-start | bytes 6291460
  3.8 0.8 copy-start.3
  4.6 0.7 copy-start.4
  5.3 0.7 copy-start.5
  6.0 0.7 copy-start.6
  6.7 0.7 copy-start.7
  56.8 2.2 %copy-start = (f32[8192,128]{1,0:T(8,128)S(1)}, f32[8192,128]{1,0:T(8,128)}, u32[]{:S(2)}) copy-start(f32[8192,128]{1,0:T(8,128)} %get-tuple-element.11.values) | copy-start | bytes 12582916

commit v3 on v2

--- a/solution.py
+++ b/solution.py
@@ -12,6 +12,7 @@
 B = 128
 SUB = 32
 UNROLL = 16
+ALL_VMEM = 60 * 2**20
 PARTS = B // SUB
 HIGH = lax.Precision.HIGHEST
 MESH = pl.DeviceIdType.MESH
@@ -51,13 +52,15 @@
     return jnp.broadcast_to(row, (B, B)).T
 
 
-def batched(count, size, one):
+def batched(count, size, one, then=None):
     def body(g, _):
         stores = []
         for i in range(size):
             stores += one(g * size + i)
         for ref, where, value in stores:
             ref[where] = value
+        if then is not None:
+            then(g)
         return 0
 
     lax.fori_loop(0, count // size, body, 0)
@@ -70,10 +73,10 @@
 def front_kernel(
     n, lanes_n, rank,
     weights, decay, marks, gaps, src, exc, base,
-    values, grad_base, minus, marks_out,
+    values_out, grad_base, minus, marks_out,
     factors, table, rows, smarks, own, gshard, u, te, ts, sym, inside, excitation, lanes, states, sums, dec, base_e,
     inverse, remain, ends, device, summaries, partial, total, back, behind, base_own, base_parts,
-    load_sem, mark_sem, ag_send, ag_recv, f_send, f_recv, p_send, p_recv, b_send, b_recv, g_send, g_recv,
+    load_sem, mark_sem, ag_send, ag_recv, f_send, f_recv, p_send, p_recv, b_send, b_recv, g_send, g_recv, values, out_sem,
 ):
     count = decay.shape[0]
     width = count * PARTS
@@ -420,7 +423,11 @@
         )
         return [(values, (s, slice(None)), jnp.where(lane < edge, excitation[s, :] * turned(ir), value))]
 
-    batched(blocks, UNROLL, feedback)
+    def piece(g):
+        s = rows_at(g, UNROLL * B)
+        return pltpu.make_async_copy(values.at[s, :], values_out.at[s, :], out_sem.at[g])
+
+    batched(blocks, UNROLL, feedback, lambda g: piece(g).start())
 
     for copy in base_copies:
         copy.wait()
@@ -435,24 +442,29 @@
             for a in range(2):
                 shard_copy(a, i, slot, p).wait_send()
 
-
-def scatter_kernel(marks, values, out, *tables):
-    count = len(tables) + 1
-    every = (out,) + tables
+    for g in range(blocks // UNROLL):
+        piece(g).wait()
+
+
+def scatter_kernel(marks, values_in, out, values, load_sem, out_sem, *tables):
+    count = len(tables)
     types = out.shape[0]
+    load = pltpu.make_async_copy(values_in, values, load_sem.at[0])
+    load.start()
 
     def zero(i, _):
-        for t in every:
-            t[pl.ds(pl.multiple_of(i * 32, 32), 32), :] = jnp.zeros((32, B), F32)
+        for t in tables:
+            t[rows_at(i, 32), :] = jnp.zeros((32, B), F32)
         return 0
 
     lax.fori_loop(0, types // 32, zero, 0)
+    load.wait()
     shards, blocks, _ = marks.shape
     for j in range(shards):
 
         def block(b, _):
             for i in range(B):
-                t = every[i % count]
+                t = tables[i % count]
                 m = marks[j, b, i]
                 e = (j * blocks + b) * B + i
                 t[pl.ds(m, 1), :] = t[pl.ds(m, 1), :] + values[pl.ds(e, 1), :]
@@ -460,18 +472,32 @@
 
         lax.fori_loop(0, blocks, block, 0)
 
-    def add(i, _):
-        s = pl.ds(pl.multiple_of(i * 32, 32), 32)
-        acc = out[s, :]
-        for t in tables:
-            acc = acc + t[s, :]
-        out[s, :] = acc
+    pieces = out_sem.shape[0]
+    size = types // pieces
+
+    def piece(c):
+        s = rows_at(c, size)
+        return pltpu.make_async_copy(tables[0].at[s, :], out.at[s, :], out_sem.at[c])
+
+    def total(c, _):
+        def add(i, _):
+            s = pl.ds(pl.multiple_of(c * size + i * 32, 32), 32)
+            acc = [t[s, :] for t in tables]
+            while len(acc) > 1:
+                acc = [acc[i] + acc[i + 1] for i in range(0, len(acc), 2)]
+            tables[0][s, :] = acc[0]
+            return 0
+
+        lax.fori_loop(0, size // 32, add, 0, unroll=2)
+        piece(c).start()
         return 0
 
-    lax.fori_loop(0, types // 32, add, 0)
-
-
-def ring_kernel(n, factor, minus, dense, grad_excite, grad_source, slots, pieces, twin_in, send, recv, t_send, t_recv):
+    lax.fori_loop(0, pieces, total, 0)
+    for c in range(pieces):
+        piece(c).wait()
+
+
+def ring_kernel(n, factor, minus, source, grad_excite, grad_source, dense, load_sem, slots, pieces, twin_in, send, recv, t_send, t_recv):
     half = n // 2
     per = dense.shape[0] // n
     rows = per // 2
@@ -489,6 +515,8 @@
         return 2 * c + lax.div(c, half // 2) * (2 * half - 1 - 4 * c)
 
     towards = [member(at + 1) + r * half, member(at - 1) + r * half]
+    load = pltpu.make_async_copy(source, dense, load_sem.at[0])
+    load.start()
     barrier = pltpu.get_barrier_semaphore()
     for p in towards + [twin]:
         pl.semaphore_signal(barrier, inc=1, device_id={"tm": p}, device_id_type=MESH)
@@ -509,7 +537,8 @@
 
     chains = range(4)
     for j in chains:
-        copy(j, 0, dense.at[span(j, 0), :]).start()
+        copy(j, 0, source.at[span(j, 0), :]).start()
+    load.wait()
 
     def step(s, _):
         for j in chains:
@@ -554,6 +583,125 @@
     lax.fori_loop(0, half - 1, sent, 0)
     for j in range(2):
         twin_copy(j).wait_send()
+
+
+def square_kernel(
+    n, factor, minus, source, grad_excite, grad_source,
+    dense, load_sem, first, second, pieces, twin_in, a_send, a_recv, b_send, b_recv, t_send, t_recv,
+):
+    half = n // 2
+    per = source.shape[0] // n
+    rows = per // 4
+    edge = B // 2
+    ranks = grad_excite.shape[0] // 2
+    me = lax.axis_index("tm")
+    r = lax.div(me, half)
+    q = lax.rem(me, half)
+    qa, qb = lax.div(q, 2), lax.rem(q, 2)
+    near = r * half + qa * 2 + 1 - qb
+    far = r * half + (1 - qa) * 2 + qb
+    twin = q + (1 - r) * half
+    load = pltpu.make_async_copy(source, dense, load_sem.at[0])
+    load.start()
+    barrier = pltpu.get_barrier_semaphore()
+    for p in (near, far, twin):
+        pl.semaphore_signal(barrier, inc=1, device_id={"tm": p}, device_id_type=MESH)
+    pl.semaphore_wait(barrier, 3)
+
+    def span(j, a, b):
+        block = a * 2 + b + ((1 - r) if j < 4 else r) * half
+        return pl.ds(pl.multiple_of(block * per + (j % 4) * rows, 8), rows)
+
+    def across(j):
+        return j % 4 == 3
+
+    def place(j, k, theirs):
+        if across(j):
+            return span(j, 1 - qa if theirs else qa, qb if k else 1 - qb)
+        return span(j, qa if k else 1 - qa, 1 - qb if theirs else qb)
+
+    def copy_a(j, k):
+        return pltpu.make_async_remote_copy(
+            src_ref=source.at[place(j, k, True), :], dst_ref=first.at[j, k],
+            send_sem=a_send.at[j, k], recv_sem=a_recv.at[j, k],
+            device_id={"tm": far if across(j) else near}, device_id_type=MESH,
+        )
+
+    def copy_b(j):
+        return pltpu.make_async_remote_copy(
+            src_ref=first.at[j, 0], dst_ref=second.at[j], send_sem=b_send.at[j], recv_sem=b_recv.at[j],
+            device_id={"tm": near if across(j) else far}, device_id_type=MESH,
+        )
+
+    def copy_t(j):
+        return pltpu.make_async_remote_copy(
+            src_ref=pieces.at[j], dst_ref=twin_in.at[j], send_sem=t_send.at[j], recv_sem=t_recv.at[j],
+            device_id={"tm": twin}, device_id_type=MESH,
+        )
+
+    def begin(j):
+        for k in range(2):
+            copy_a(j, k).start()
+
+    def middle(j):
+        copy_a(j, 0).wait_recv()
+        first[j, 0] = first[j, 0] + dense[place(j, 0, False), :]
+        copy_b(j).start()
+        copy_a(j, 1).wait_recv()
+
+    def put(value, j, who):
+        for i in range(rows // B):
+            t = value[i * B : (i + 1) * B].T
+            lanes = slice((j % 4) * rows + i * B, (j % 4) * rows + (i + 1) * B)
+            at = pl.ds(pl.multiple_of(who * ranks, ranks), ranks)
+            grad_excite[at, lanes] = t[:ranks]
+            grad_source[at, lanes] = t[edge : edge + ranks]
+
+    def last(j):
+        copy_b(j).wait_recv()
+        value = (second[j] + first[j, 1] + dense[place(j, 1, False), :]) * factor - minus[0:1, :]
+        if j < 4:
+            pieces[j] = value
+            copy_t(j).start()
+        else:
+            put(value, j, r)
+
+    begin(0)
+    begin(3)
+    begin(1)
+    load.wait()
+    middle(0)
+    begin(2)
+    middle(3)
+    begin(7)
+    middle(1)
+    begin(4)
+    last(0)
+    middle(2)
+    begin(5)
+    last(3)
+    last(1)
+    middle(4)
+    begin(6)
+    last(2)
+    middle(7)
+    middle(5)
+    last(4)
+    last(7)
+    middle(6)
+    last(5)
+    for j in (0, 3, 1):
+        copy_t(j).wait_recv()
+        put(twin_in[j], j, 1 - r)
+    last(6)
+    copy_t(2).wait_recv()
+    put(twin_in[2], 2, 1 - r)
+    for j in range(8):
+        for k in range(2):
+            copy_a(j, k).wait_send()
+        copy_b(j).wait_send()
+    for j in range(4):
+        copy_t(j).wait_send()
 
 
 def body(marks, gaps, excite, source, base_rate, weights, decay):
@@ -586,7 +734,7 @@
             jax.ShapeDtypeStruct((2, shard_blocks, B), jnp.int32),
         ],
         in_specs=[SMEM, SMEM, VMEM, VMEM, HBM, HBM, VMEM],
-        out_specs=[VMEM] * 4,
+        out_specs=[HBM] + [VMEM] * 3,
         scratch_shapes=[
             pltpu.VMEM((B, types), BF16),
             pltpu.VMEM((types, B), F32),
@@ -611,9 +759,10 @@
             dma((2 * lanes_n - 1,)), dma((2 * lanes_n - 1,)),
             dma((half - 1,)), dma((half - 1,)),
             dma((n - 1,)), dma((n - 1,)),
+            tall, dma((blocks // UNROLL,)),
         ],
         compiler_params=pltpu.CompilerParams(
-            collective_id=0, has_side_effects=True, vmem_limit_bytes=48 * 2**20
+            collective_id=0, has_side_effects=True, vmem_limit_bytes=ALL_VMEM
         ),
     )(weights, decay, marks.reshape(shard_blocks, B), gaps.reshape(shard_blocks, B), source, excite,
       base_rate.reshape(groups, B))
@@ -621,25 +770,38 @@
     dense = pl.pallas_call(
         scatter_kernel,
         out_shape=jax.ShapeDtypeStruct((types, B), F32),
-        in_specs=[SMEM, VMEM],
-        out_specs=VMEM,
-        scratch_shapes=[pltpu.VMEM((types, B), F32)] * 7,
-        compiler_params=pltpu.CompilerParams(vmem_limit_bytes=40 * 2**20),
+        in_specs=[SMEM, HBM],
+        out_specs=HBM,
+        scratch_shapes=[tall, dma((1,)), dma((8,))] + [pltpu.VMEM((types, B), F32)] * 8,
+        compiler_params=pltpu.CompilerParams(vmem_limit_bytes=ALL_VMEM),
     )(marks_all, values)
 
-    grad_excite, grad_source = pl.pallas_call(
-        functools.partial(ring_kernel, n, types / (events * half)),
-        out_shape=[jax.ShapeDtypeStruct((slices, types_own), F32)] * 2,
-        in_specs=[VMEM] * 2,
-        out_specs=[VMEM] * 2,
-        scratch_shapes=[
+    quarter = types_own // 4
+    if half == 4 and quarter % B == 0:
+        kernel = square_kernel
+        scratch = [
+            pltpu.VMEM((8, 2, quarter, B), F32),
+            pltpu.VMEM((8, quarter, B), F32),
+            pltpu.VMEM((4, quarter, B), F32),
+            pltpu.VMEM((4, quarter, B), F32),
+            dma((8, 2)), dma((8, 2)), dma((8,)), dma((8,)), dma((4,)), dma((4,)),
+        ]
+    else:
+        kernel = ring_kernel
+        scratch = [
             pltpu.VMEM((4, half - 1, types_own // 2, B), F32),
             pltpu.VMEM((4, types_own // 2, B), F32),
             pltpu.VMEM((2, types_own // 2, B), F32),
             dma((4, half - 1)), dma((4, half - 1)), dma((2,)), dma((2,)),
-        ],
+        ]
+    grad_excite, grad_source = pl.pallas_call(
+        functools.partial(kernel, n, types / (events * half)),
+        out_shape=[jax.ShapeDtypeStruct((slices, types_own), F32)] * 2,
+        in_specs=[VMEM, HBM],
+        out_specs=[VMEM] * 2,
+        scratch_shapes=[pltpu.VMEM((types, B), F32), dma((1,))] + scratch,
         compiler_params=pltpu.CompilerParams(
-            collective_id=1, has_side_effects=True, vmem_limit_bytes=40 * 2**20
+            collective_id=1, has_side_effects=True, vmem_limit_bytes=52 * 2**20
         ),
     )(minus, dense)
     return grad_excite, grad_source, grad_base.reshape(types_own)

time: 129 us -> 113 us (0.88)
  local copies, waits for them, and re-layouts: 11 us -> 2.19 us
  Pallas kernels: 117 us -> 110 us
    unnamed x19 -> x7, local copies, waits for them, and re-layouts: 11 us -> 2.19 us
    pallas_call x1, Pallas kernels: 54 us -> 47.8 us  [body(): pl.pallas_call(functools.partial(kernel, n, types / (events * half)), out...]
where the time goes in v3:
time: 113 us
  Pallas kernels  110 us (97%)
  local copies, waits for them, and re-layouts  2.19 us (2%)
    pallas_call x1, Pallas kernels, body(): pl.pallas_call(functools.partial(front_kernel, n, lanes_n, rank), out_sha...  48.4 us
    pallas_call x1, Pallas kernels, body(): pl.pallas_call(functools.partial(kernel, n, types / (events * half)), out...  47.8 us
    pallas_call x1, Pallas kernels, body(): pl.pallas_call(scatter_kernel, out_shape=jax.ShapeDtypeStruct((types, B),...  13.7 us

profile of v3, /device:TPU:0, one launch (start us, length us, event | category | flops | bytes accessed | tf_op | source)
XLA Modules:
  0.0 112.8 jit_solution(13167439651075024683)
XLA Ops:
  0.6 48.4 %shard_map.94 = (f32[8192,128]{1,0:T(8,128)}, f32[8,128]{1,0:T(8,128)}, f32[8,128]{1,0:T(8,128)}, s32[2,32,128]{2,1,0:T(8,128)}) custom-call(f32[8]{0:T(128)} %weights.1, f32[8]{0:T(128)} %decay.1, s32[32,128]{1,0:T(8,128)} %bitcast.5, s32[32,128]{1,0:T(8,128)} %bitcast.6, bf16[128,8192]{1,0:T(8,128)(2,1)} %src.1, bf16[128,8192]{1,0:T(8,128)(2,1)} %exc.1, ...), custom_call_target="tpu_custom_call" | custom-call | tf_op jit(solution)/shard_map/pallas_call | solution.py:728
  49.1 0.0 copy-start
  49.1 13.7 %shard_map.95.source = f32[8192,128]{1,0:T(8,128)} custom-call(s32[2,32,128]{2,1,0:T(8,128)} %get-tuple-element.10.marks, f32[8192,128]{1,0:T(8,128)} %get-tuple-element.11.values_in), custom_call_target="tpu_custom_call" | custom-call | tf_op jit(solution)/shard_map/pallas_call | solution.py:770
  62.8 0.0 copy-done
  62.8 0.0 copy-start.1
  62.8 47.8 %shard_map.96 = (f32[128,1024]{1,0:T(8,128)S(1)}, f32[128,1024]{1,0:T(8,128)S(1)}) custom-call(f32[8,128]{1,0:T(8,128)S(1)} %copy-done, f32[8192,128]{1,0:T(8,128)} %shard_map.95.source), custom_call_target="tpu_custom_call" | custom-call | tf_op jit(solution)/shard_map/pallas_call | solution.py:797
  110.6 0.8 copy.13
  111.4 0.8 copy.14
  112.2 0.0 copy-done.1
  112.2 0.6 copy.15
Async XLA Ops:
  49.1 13.8 %copy-start = (f32[8,128]{1,0:T(8,128)S(1)}, f32[8,128]{1,0:T(8,128)}, u32[]{:S(2)}) copy-start(f32[8,128]{1,0:T(8,128)} %get-tuple-element.9.minus) | copy-start | bytes 12292
  62.8 49.4 %copy-start.1 = (f32[8,128]{1,0:T(8,128)S(1)}, f32[8,128]{1,0:T(8,128)}, u32[]{:S(2)}) copy-start(f32[8,128]{1,0:T(8,128)} %get-tuple-element.14) | copy-start | bytes 12292

commit v4 on v3

--- a/solution.py
+++ b/solution.py
@@ -116,28 +116,19 @@
         pl.semaphore_signal(barrier, inc=1, device_id=t, device_id_type=MESH)
     pl.semaphore_wait(barrier, len(targets))
 
-    slot = lax.rem(me, 2)
     own[...] = marks[...]
-
-    def shard_copy(a, i, j, target):
-        ref, dst = ((own, marks_out), (gaps, gshard))[a]
-        return pltpu.make_async_remote_copy(
-            src_ref=ref, dst_ref=dst.at[j], send_sem=ag_send.at[a, i], recv_sem=ag_recv.at[a, j],
-            device_id={"tm": target}, device_id_type=MESH,
+    marks_out[r] = marks[...]
+    gshard[r] = gaps[...]
+    first_move = pltpu.make_async_copy(own, smarks.at[r], mark_sem.at[0])
+    first_move.start()
+    gathers = []
+    for a, (ref, dst) in enumerate(((own, marks_out), (gaps, gshard))):
+        copy = pltpu.make_async_remote_copy(
+            src_ref=ref, dst_ref=dst.at[r], send_sem=ag_send.at[a], recv_sem=ag_recv.at[a],
+            device_id={"tm": twin}, device_id_type=MESH,
         )
-
-    dests = [lax.div(me, 2) + i * half for i in range(2)]
-    for i, p in enumerate(dests):
-
-        @pl.when(p != me)
-        def _():
-            for a in range(2):
-                shard_copy(a, i, slot, p).start()
-
-        @pl.when(p == me)
-        def _():
-            marks_out[slot] = marks[...]
-            gshard[slot] = gaps[...]
+        copy.start()
+        gathers.append(copy)
 
     for copy in loads:
         copy.wait()
@@ -151,54 +142,42 @@
     acc = lax.fori_loop(0, groups, build, jnp.zeros((8, B), F32), unroll=8)
     xtot = jnp.sum(acc, axis=0, keepdims=True)
 
-    for j in range(2):
-
-        @pl.when(2 * q + j != me)
-        def _():
-            for a in range(2):
-                shard_copy(a, 0, j, twin).wait_recv()
-
-    move = pltpu.make_async_copy(marks_out, smarks, mark_sem.at[0])
-    move.start()
-
     d8, w8 = down(decay, count), down(weights, count)
-    gap_all = jnp.concatenate([gshard[0], gshard[1]], 0).astype(F32)
     li, lj = iota((B, B), 0), iota((B, B), 1)
-    first = lax.div(lj, SUB) * SUB
+    start_lane = lax.div(lj, SUB) * SUB
+    part_row = lax.div(iota((1, B), 1), SUB)
+    lane = iota((1, B), 1)
 
     def pick(mask, a):
         return jnp.dot(a, mask.astype(F32), precision=HIGH, preferred_element_type=F32)
-
-    uv = pick(li <= lj, gap_all)
-    u[...] = uv
-    te[...] = pick(li <= first + SUB - 1, gap_all)
-    ts[...] = pick(li < first, gap_all)
-    lengths = jnp.broadcast_to(uv[:, B - 1 :], (blocks, B))
-    after_mask = (iota((blocks, blocks), 1) > iota((blocks, blocks), 0)).astype(F32)
-    endv = jnp.dot(after_mask, lengths, precision=HIGH, preferred_element_type=F32)
-    ends[...] = endv
-    duration = endv[0:1, :] + lengths[0:1, :]
-    move.wait()
-
-    for j in range(2):
-
-        def fetch(g, _):
-            for i in range(B):
-                m = smarks[j, g, i]
-                e = (j * shard_blocks + g) * B + i
-                rows[pl.ds(e, 1), :] = table[pl.ds(m, 1), :]
-            return 0
-
-        lax.fori_loop(0, shard_blocks, fetch, 0)
-
-    part_row = lax.div(iota((1, B), 1), SUB)
-    lane = iota((1, B), 1)
 
     def two(a, b):
         k = a.shape[0]
         high, low = halves(a)
         both = dot(jnp.concatenate([high, low], 0).astype(BF16), b)
         return both[:k] + both[k:]
+
+    def prepare(j):
+        gap = gshard[j].astype(F32)
+        uv = pick(li <= lj, gap)
+        at = rows_at(j, shard_blocks)
+        u[at, :] = uv
+        te[at, :] = pick(li <= start_lane + SUB - 1, gap)
+        ts[at, :] = pick(li < start_lane, gap)
+        lengths = jnp.broadcast_to(uv[:, B - 1 :], (shard_blocks, B))
+        later = (iota((shard_blocks, shard_blocks), 1) > iota((shard_blocks, shard_blocks), 0)).astype(F32)
+        left = jnp.dot(later, lengths, precision=HIGH, preferred_element_type=F32)
+        ends[at, :] = left
+        device[j, count:, :] = jnp.broadcast_to(left[0:1, :] + lengths[0:1, :], (8, B))
+
+    def fetch(j):
+        def block(b, _):
+            for i in range(B):
+                m = smarks[j, b, i]
+                rows[pl.ds((j * shard_blocks + b) * B + i, 1), :] = table[pl.ds(m, 1), :]
+            return 0
+
+        lax.fori_loop(0, shard_blocks, block, 0)
 
     def emit(b):
         ur, er, sr = u[pl.ds(b, 1), :], te[pl.ds(b, 1), :], ts[pl.ds(b, 1), :]
@@ -211,18 +190,35 @@
             (dec, spot, jnp.concatenate([jnp.broadcast_to(t, (count, B)) for t in decays], 0)),
         ]
 
-    batched(blocks, UNROLL, emit)
-
-    def forward_state(start, keep):
-        def step(b, state):
-            for c in range(PARTS):
-                s = pl.ds(pl.multiple_of(b * width + c * count, count), count)
-                if keep:
-                    states[s, :] = state
-                state = state * dec[s, :] + sums[s, :]
-            return state
-
-        return lax.fori_loop(0, blocks, step, start, unroll=2)
+    prepare(r)
+    first_move.wait()
+    fetch(r)
+    batched(shard_blocks, UNROLL, lambda b: emit(r * shard_blocks + b))
+    for copy in gathers:
+        copy.wait_recv()
+    second_move = pltpu.make_async_copy(marks_out.at[1 - r], smarks.at[1 - r], mark_sem.at[1])
+    second_move.start()
+    prepare(1 - r)
+    second_move.wait()
+    fetch(1 - r)
+    batched(shard_blocks, UNROLL, lambda b: emit((1 - r) * shard_blocks + b))
+
+    zero = jnp.zeros((count, B), F32)
+
+    def recur(start, keep, ahead):
+        def step(i, pair):
+            b = i if ahead else shard_blocks - 1 - i
+            for c in range(PARTS) if ahead else reversed(range(PARTS)):
+                nxt = []
+                for j in range(2):
+                    s = pl.ds(pl.multiple_of((j * shard_blocks + b) * width + c * count, count), count)
+                    if keep:
+                        states[s, :] = pair[j]
+                    nxt.append(pair[j] * dec[s, :] + sums[s, :])
+                pair = tuple(nxt)
+            return pair
+
+        return lax.fori_loop(0, shard_blocks, step, start, unroll=2)
 
     def share(source, dest, send, recv):
         copies = []
@@ -238,8 +234,8 @@
         dest[q] = source[...]
         return copies
 
-    device[0:count, :] = forward_state(jnp.zeros((count, B), F32), False)
-    device[count:, :] = jnp.broadcast_to(duration, (count, B))
+    for j, state in enumerate(recur((zero, zero), False, True)):
+        device[j, 0:count, :] = state
     state_copies = share(device, summaries, f_send, f_recv)
 
     base_high, base_low = halves(base[...])
@@ -281,47 +277,59 @@
 
     for copy in state_copies:
         copy.wait()
-    start = jnp.zeros((count, B), F32)
-    after = jnp.zeros((1, B), F32)
+    start = [zero, zero]
+    after = [jnp.zeros((1, B), F32)] * 2
     t_end = jnp.zeros((1, B), F32)
-    for p in range(half):
-        span = summaries[p, count : count + 1, :]
-        start = jnp.where(p < q, start * jnp.exp(-d8 * span) + summaries[p, 0:count, :], start)
-        after = after + jnp.where(p > q, span, 0.0)
+    for t in range(n):
+        held = summaries[t % half, t // half]
+        span = held[count : count + 1]
         t_end = t_end + span
-    forward_state(start, True)
-
-    ones = jnp.ones((8, B), BF16)
+        for j in range(2):
+            mark = q + j * half
+            start[j] = jnp.where(t < mark, start[j] * jnp.exp(-d8 * span) + held[0:count], start[j])
+            after[j] = after[j] + jnp.where(t > mark, span, 0.0)
+    recur(tuple(start), True, True)
+    for j in range(2):
+        at = slice(j * shard_blocks, (j + 1) * shard_blocks)
+        ends[at, :] = ends[at, :] + after[j]
+
     fill = jnp.zeros((B - 3 * width, B), F32)
 
     def forward(b):
         s = rows_at(b, B)
         sh, sl = halves(states[rows_at(b, width), :])
         value = inside[s, :] + dot(lanes[s, :], jnp.concatenate([sh, sl, sh, fill], 0).astype(BF16))
-        product = jnp.where(lane < edge, value * pltpu.roll(rows[s, :], edge, 1), 0.0)
-        high, low = halves(product)
-        tot = lax.dot_general(ones, high.astype(BF16), NT, preferred_element_type=F32)
-        tot = tot + lax.dot_general(ones, low.astype(BF16), NT, preferred_element_type=F32)
+        product = value * pltpu.roll(rows[s, :], edge, 1)
+        tot = jnp.sum(product.T[:edge], axis=0, keepdims=True)
         return [
             (excitation, (s, slice(None)), value),
-            (partial, (pl.ds(b, 1), slice(None)), tot[0:1, :] * (1.0 / rank)),
+            (partial, (pl.ds(b, 1), slice(None)), tot * (1.0 / rank)),
         ]
 
-    batched(blocks, UNROLL, forward)
-
     spot = mine * 2 + r
-    part_copies = []
-    for i, t in enumerate([(twin, mine)] + [(t, o) for o in others for t in (me, twin)]):
-        copy = pltpu.make_async_remote_copy(
-            src_ref=partial, dst_ref=total.at[spot], send_sem=p_send.at[i], recv_sem=p_recv.at[i],
-            device_id={"tm": t[0], "mark": t[1]}, device_id_type=MESH,
-        )
-        copy.start()
-        part_copies.append(copy)
+
+    def part_copies(g):
+        s = rows_at(g, UNROLL)
+        copies = []
+        for i, t in enumerate([(twin, mine)] + [(t, o) for o in others for t in (me, twin)]):
+            copies.append(
+                pltpu.make_async_remote_copy(
+                    src_ref=partial.at[s, :], dst_ref=total.at[spot, s, :],
+                    send_sem=p_send.at[i, g], recv_sem=p_recv.at[i, g],
+                    device_id={"tm": t[0], "mark": t[1]}, device_id_type=MESH,
+                )
+            )
+        return copies
+
+    def send_part(g):
+        for copy in part_copies(g):
+            copy.start()
+
+    batched(blocks, UNROLL, forward, send_part)
     total[spot] = partial[...]
 
     def rest(b, comp):
-        left = w8 * (1.0 - jnp.exp(-d8 * (u[pl.ds(b, 1), :] * -1.0 + lengths_row(b) + ends[pl.ds(b, 1), :] + after)))
+        left = w8 * (1.0 - jnp.exp(-d8 * (u[pl.ds(b, 1), :] * -1.0 + lengths_row(b) + ends[pl.ds(b, 1), :])))
         rem = jnp.sum(left, axis=0, keepdims=True)
         remain[pl.ds(b, 1), :] = rem
         return comp + two(jnp.broadcast_to(rem, (8, B)), rows[rows_at(b, B), :].astype(BF16))
@@ -331,8 +339,9 @@
 
     comp = lax.fori_loop(0, blocks, rest, jnp.zeros((8, B), F32), unroll=4)
 
-    for copy in part_copies:
-        copy.wait()
+    for g in range(blocks // UNROLL):
+        for copy in part_copies(g):
+            copy.wait()
     intensity = base_e[...]
     for j in range(2 * lanes_n):
         intensity = intensity + total[j]
@@ -344,20 +353,9 @@
 
     batched(blocks, UNROLL, reverse)
 
-    def reverse_state(start, keep):
-        def step(i, state):
-            b = blocks - 1 - i
-            for c in reversed(range(PARTS)):
-                s = pl.ds(pl.multiple_of(b * width + c * count, count), count)
-                if keep:
-                    states[s, :] = state
-                state = state * dec[s, :] + sums[s, :]
-            return state
-
-        return lax.fori_loop(0, blocks, step, start, unroll=2)
-
-    behind[0:count, :] = reverse_state(jnp.zeros((count, B), F32), False)
-    behind[count:, :] = comp
+    for j, state in enumerate(recur((zero, zero), False, False)):
+        behind[j * count : (j + 1) * count, :] = state
+    behind[2 * count :, :] = comp
     back_copies = share(behind, back, b_send, b_recv)
 
     def spread(i, both):
@@ -382,15 +380,32 @@
         base_copies.append(copy)
     base_parts[me] = base_own[me]
 
+    def feedback(b):
+        s = rows_at(b, B)
+        ir = inverse[pl.ds(b, 1), :]
+        high, low = halves(jnp.where(subi < subj, sym[rows_at(b, SUB), :] * ir, 0.0))
+        left = jnp.concatenate([parted(high), parted(low)], 0).astype(BF16)
+        both = dot(left, rows[s, :].astype(BF16))
+        return [(inside, (s, slice(None)), jnp.where(lane < edge, excitation[s, :] * turned(ir), both[:B] + both[B:]))]
+
+    batched(blocks, UNROLL, feedback)
+
     for copy in back_copies:
         copy.wait()
-    pending = jnp.zeros((count, B), F32)
+    pending = [zero, zero]
     comp_all = jnp.zeros((8, B), F32)
-    for p in reversed(range(half)):
-        span = summaries[p, count : count + 1, :]
-        pending = jnp.where(p > q, pending * jnp.exp(-d8 * span) + back[p, 0:count, :], pending)
-        comp_all = comp_all + back[p, count:, :]
-    reverse_state(pending, True)
+    for p in range(half):
+        comp_all = comp_all + back[p, 2 * count :, :]
+    for t in reversed(range(n)):
+        p, k = t % half, t // half
+        span = summaries[p, k, count : count + 1, :]
+        for j in range(2):
+            pending[j] = jnp.where(
+                t > q + j * half,
+                pending[j] * jnp.exp(-d8 * span) + back[p, k * count : (k + 1) * count, :],
+                pending[j],
+            )
+    recur(tuple(pending), True, False)
     events_all = blocks * B * half
     minus[...] = jnp.where(lane < edge, comp_all * (1.0 / events_all), 0.0)
 
@@ -408,26 +423,21 @@
     xstack = thirds(xtot * (-1.0 / types), ((0, 2, 5), (1, 4), (3,)))
     fill24 = jnp.zeros((B - 3 * width - 8, B), F32)
 
-    def feedback(b):
+    def distant(b):
         s = rows_at(b, B)
-        ur, er, ir = u[pl.ds(b, 1), :], te[pl.ds(b, 1), :], inverse[pl.ds(b, 1), :]
-        high, low = halves(jnp.where(subi < subj, sym[rows_at(b, SUB), :] * ir, 0.0))
-        left = jnp.concatenate([parted(high), parted(low)], 0).astype(BF16)
-        both = dot(left, rows[s, :].astype(BF16))
-        lh, ll = halves(parted(w8 * jnp.exp(-d8 * (er - ur))))
+        lh, ll = halves(parted(w8 * jnp.exp(-d8 * (te[pl.ds(b, 1), :] - u[pl.ds(b, 1), :]))))
         rstack = thirds(remain[pl.ds(b, 1), :], ((0, 1, 3), (2, 4), (5,)))
         turn = jnp.concatenate([lh, lh, ll, rstack, fill24], 0).T.astype(BF16)
         sh, sl = halves(states[rows_at(b, width), :])
-        value = both[:B] + both[B:] + dot(
-            turn, jnp.concatenate([sh, sl, sh, xstack, fill24], 0).astype(BF16)
-        )
-        return [(values, (s, slice(None)), jnp.where(lane < edge, excitation[s, :] * turned(ir), value))]
+        stack = jnp.concatenate([sh, sl, sh, xstack, fill24], 0)
+        value = dot(turn, jnp.where(lane < edge, 0.0, stack).astype(BF16))
+        return [(values, (s, slice(None)), inside[s, :] + value)]
 
     def piece(g):
         s = rows_at(g, UNROLL * B)
         return pltpu.make_async_copy(values.at[s, :], values_out.at[s, :], out_sem.at[g])
 
-    batched(blocks, UNROLL, feedback, lambda g: piece(g).start())
+    batched(blocks, UNROLL, distant, lambda g: piece(g).start())
 
     for copy in base_copies:
         copy.wait()
@@ -435,13 +445,8 @@
     for p in range(1, n):
         base_all = base_all + base_parts[p]
     grad_base[...] = base_all * (types / events_all) - t_end * (1.0 / events_all)
-    for i, p in enumerate(dests):
-
-        @pl.when(p != me)
-        def _():
-            for a in range(2):
-                shard_copy(a, i, slot, p).wait_send()
-
+    for copy in gathers:
+        copy.wait_send()
     for g in range(blocks // UNROLL):
         piece(g).wait()
 
@@ -647,7 +652,6 @@
         copy_a(j, 0).wait_recv()
         first[j, 0] = first[j, 0] + dense[place(j, 0, False), :]
         copy_b(j).start()
-        copy_a(j, 1).wait_recv()
 
     def put(value, j, who):
         for i in range(rows // B):
@@ -658,6 +662,7 @@
             grad_source[at, lanes] = t[edge : edge + ranks]
 
     def last(j):
+        copy_a(j, 1).wait_recv()
         copy_b(j).wait_recv()
         value = (second[j] + first[j, 1] + dense[place(j, 1, False), :]) * factor - minus[0:1, :]
         if j < 4:
@@ -666,26 +671,34 @@
         else:
             put(value, j, r)
 
-    begin(0)
-    begin(3)
-    begin(1)
+    copy_a(0, 0).start()
+    copy_a(3, 0).start()
+    copy_a(1, 0).start()
+    copy_a(0, 1).start()
+    copy_a(3, 1).start()
     load.wait()
     middle(0)
-    begin(2)
+    copy_a(2, 0).start()
+    copy_a(1, 1).start()
     middle(3)
-    begin(7)
+    copy_a(7, 0).start()
     middle(1)
-    begin(4)
+    copy_a(4, 0).start()
+    copy_a(2, 1).start()
     last(0)
     middle(2)
-    begin(5)
+    copy_a(5, 0).start()
+    copy_a(7, 1).start()
     last(3)
     last(1)
     middle(4)
-    begin(6)
+    copy_a(6, 0).start()
+    copy_a(4, 1).start()
     last(2)
     middle(7)
     middle(5)
+    copy_a(5, 1).start()
+    copy_a(6, 1).start()
     last(4)
     last(7)
     middle(6)
@@ -721,8 +734,6 @@
     plane = pltpu.VMEM((blocks, B), F32)
     tall = pltpu.VMEM((events, B), F32)
     small = pltpu.VMEM((blocks * width, B), F32)
-    packet = pltpu.VMEM((count + 8, B), F32)
-    packets = pltpu.VMEM((half, count + 8, B), F32)
     types_own = types // n
 
     values, grad_base, minus, marks_all = pl.pallas_call(
@@ -748,15 +759,15 @@
             pltpu.VMEM((events, B), BF16),
             small, small, small,
             plane, plane, plane, plane,
-            packet, packets,
+            pltpu.VMEM((2, count + 8, B), F32), pltpu.VMEM((half, 2, count + 8, B), F32),
             plane, pltpu.VMEM((2 * lanes_n, blocks, B), F32),
-            packets, packet,
+            pltpu.VMEM((half, 2 * count + 8, B), F32), pltpu.VMEM((2 * count + 8, B), F32),
             pltpu.VMEM((n, groups // n, B), F32),
             pltpu.VMEM((n, groups // n, B), F32),
-            dma((2,)), dma((1,)),
-            dma((2, 2)), dma((2, 2)),
+            dma((2,)), dma((2,)),
+            dma((2,)), dma((2,)),
             dma((half - 1,)), dma((half - 1,)),
-            dma((2 * lanes_n - 1,)), dma((2 * lanes_n - 1,)),
+            dma((2 * lanes_n - 1, blocks // UNROLL)), dma((2 * lanes_n - 1, blocks // UNROLL)),
             dma((half - 1,)), dma((half - 1,)),
             dma((n - 1,)), dma((n - 1,)),
             tall, dma((blocks // UNROLL,)),

time: 113 us -> 102 us (0.903)
  Pallas kernels: 110 us -> 99 us
    pallas_call x1, Pallas kernels: 48.4 us -> 41 us  [body(): pl.pallas_call(functools.partial(front_kernel, n, lanes_n, rank), out_sha...]
    pallas_call x1, Pallas kernels: 47.8 us -> 44.2 us  [body(): pl.pallas_call(functools.partial(kernel, n, types / (events * half)), out...]
where the time goes in v4:
time: 102 us
  Pallas kernels  99 us (97%)
  local copies, waits for them, and re-layouts  2.19 us (2%)
    pallas_call x1, Pallas kernels, body(): pl.pallas_call(functools.partial(kernel, n, types / (events * half)), out...  44.2 us
    pallas_call x1, Pallas kernels, body(): pl.pallas_call(functools.partial(front_kernel, n, lanes_n, rank), out_sha...  41 us
    pallas_call x1, Pallas kernels, body(): pl.pallas_call(scatter_kernel, out_shape=jax.ShapeDtypeStruct((types, B),...  13.7 us
    unnamed x7, local copies, waits for them, and re-layouts  2.19 us

profile of v4, /device:TPU:0, one launch (start us, length us, event | category | flops | bytes accessed | tf_op | source)
XLA Modules:
  0.0 101.9 jit_solution(12937286793056140382)
XLA Ops:
  0.6 41.0 %shard_map.94 = (f32[8192,128]{1,0:T(8,128)}, f32[8,128]{1,0:T(8,128)}, f32[8,128]{1,0:T(8,128)}, s32[2,32,128]{2,1,0:T(8,128)}) custom-call(f32[8]{0:T(128)} %weights.1, f32[8]{0:T(128)} %decay.1, s32[32,128]{1,0:T(8,128)} %bitcast.5, s32[32,128]{1,0:T(8,128)} %bitcast.6, bf16[128,8192]{1,0:T(8,128)(2,1)} %src.1, bf16[128,8192]{1,0:T(8,128)(2,1)} %exc.1, ...), custom_call_target="tpu_custom_call" | custom-call | tf_op jit(solution)/shard_map/pallas_call | solution.py:739
  41.7 0.0 copy-start
  41.7 13.7 %shard_map.95.source = f32[8192,128]{1,0:T(8,128)} custom-call(s32[2,32,128]{2,1,0:T(8,128)} %get-tuple-element.10.marks, f32[8192,128]{1,0:T(8,128)} %get-tuple-element.11.values_in), custom_call_target="tpu_custom_call" | custom-call | tf_op jit(solution)/shard_map/pallas_call | solution.py:781
  55.4 0.0 copy-done
  55.4 0.0 copy-start.1
  55.4 44.2 %shard_map.96 = (f32[128,1024]{1,0:T(8,128)S(1)}, f32[128,1024]{1,0:T(8,128)S(1)}) custom-call(f32[8,128]{1,0:T(8,128)S(1)} %copy-done, f32[8192,128]{1,0:T(8,128)} %shard_map.95.source), custom_call_target="tpu_custom_call" | custom-call | tf_op jit(solution)/shard_map/pallas_call | solution.py:808
  99.7 0.8 copy.13
  100.5 0.8 copy.14
  101.3 0.0 copy-done.1
  101.3 0.6 copy.15
Async XLA Ops:
  41.7 13.8 %copy-start = (f32[8,128]{1,0:T(8,128)S(1)}, f32[8,128]{1,0:T(8,128)}, u32[]{:S(2)}) copy-start(f32[8,128]{1,0:T(8,128)} %get-tuple-element.9.minus) | copy-start | bytes 12292
  55.4 45.8 %copy-start.1 = (f32[8,128]{1,0:T(8,128)S(1)}, f32[8,128]{1,0:T(8,128)}, u32[]{:S(2)}) copy-start(f32[8,128]{1,0:T(8,128)} %get-tuple-element.14) | copy-start | bytes 12292

commit v5 on v4

--- a/solution.py
+++ b/solution.py
@@ -72,11 +72,12 @@
 
 def front_kernel(
     n, lanes_n, rank,
-    weights, decay, marks, gaps, src, exc, base,
-    values_out, grad_base, minus, marks_out,
+    weights_in, decay_in, marks_in, gaps_in, src, exc, base_in,
+    values_out, base_out, minus_out, marks_all,
     factors, table, rows, smarks, own, gshard, u, te, ts, sym, inside, excitation, lanes, states, sums, dec, base_e,
     inverse, remain, ends, device, summaries, partial, total, back, behind, base_own, base_parts,
     load_sem, mark_sem, ag_send, ag_recv, f_send, f_recv, p_send, p_recv, b_send, b_recv, g_send, g_recv, values, out_sem,
+    weights, decay, marks, gaps, base, grad_base, minus, marks_out, in_sem, end_sem,
 ):
     count = decay.shape[0]
     width = count * PARTS
@@ -99,6 +100,19 @@
     if ranks < edge:
         for a in range(2):
             factors[a * edge + ranks : (a + 1) * edge, :] = jnp.zeros((edge - ranks, types), BF16)
+    barrier = pltpu.get_barrier_semaphore()
+    targets = [{"tm": p, "mark": mine} for p in peers]
+    targets += [{"tm": t, "mark": o} for o in others for t in (me, twin)]
+    for t in targets:
+        pl.semaphore_signal(barrier, inc=1, device_id=t, device_id_type=MESH)
+    small = [
+        pltpu.make_async_copy(a, b, in_sem.at[i])
+        for i, (a, b) in enumerate(
+            ((marks_in, marks), (gaps_in, gaps), (weights_in, weights), (decay_in, decay), (base_in, base))
+        )
+    ]
+    for copy in small:
+        copy.start()
     loads = []
     for a, ref in enumerate((src, exc)):
         copy = pltpu.make_async_copy(
@@ -109,19 +123,15 @@
         copy.start()
         loads.append(copy)
 
-    barrier = pltpu.get_barrier_semaphore()
-    targets = [{"tm": p, "mark": mine} for p in peers]
-    targets += [{"tm": t, "mark": o} for o in others for t in (me, twin)]
-    for t in targets:
-        pl.semaphore_signal(barrier, inc=1, device_id=t, device_id_type=MESH)
-    pl.semaphore_wait(barrier, len(targets))
-
+    small[0].wait()
+    small[1].wait()
     own[...] = marks[...]
     marks_out[r] = marks[...]
     gshard[r] = gaps[...]
     first_move = pltpu.make_async_copy(own, smarks.at[r], mark_sem.at[0])
     first_move.start()
     gathers = []
+    pl.semaphore_wait(barrier, len(targets))
     for a, (ref, dst) in enumerate(((own, marks_out), (gaps, gshard))):
         copy = pltpu.make_async_remote_copy(
             src_ref=ref, dst_ref=dst.at[r], send_sem=ag_send.at[a], recv_sem=ag_recv.at[a],
@@ -142,6 +152,8 @@
     acc = lax.fori_loop(0, groups, build, jnp.zeros((8, B), F32), unroll=8)
     xtot = jnp.sum(acc, axis=0, keepdims=True)
 
+    for copy in small[2:]:
+        copy.wait()
     d8, w8 = down(decay, count), down(weights, count)
     li, lj = iota((B, B), 0), iota((B, B), 1)
     start_lane = lax.div(lj, SUB) * SUB
@@ -172,12 +184,13 @@
 
     def fetch(j):
         def block(b, _):
-            for i in range(B):
-                m = smarks[j, b, i]
-                rows[pl.ds((j * shard_blocks + b) * B + i, 1), :] = table[pl.ds(m, 1), :]
+            for k in range(4):
+                for i in range(B):
+                    m = smarks[j, b * 4 + k, i]
+                    rows[pl.ds((j * shard_blocks + b * 4 + k) * B + i, 1), :] = table[pl.ds(m, 1), :]
             return 0
 
-        lax.fori_loop(0, shard_blocks, block, 0)
+        lax.fori_loop(0, shard_blocks // 4, block, 0)
 
     def emit(b):
         ur, er, sr = u[pl.ds(b, 1), :], te[pl.ds(b, 1), :], ts[pl.ds(b, 1), :]
@@ -198,6 +211,8 @@
         copy.wait_recv()
     second_move = pltpu.make_async_copy(marks_out.at[1 - r], smarks.at[1 - r], mark_sem.at[1])
     second_move.start()
+    marks_copy = pltpu.make_async_copy(marks_out, marks_all, end_sem.at[0])
+    marks_copy.start()
     prepare(1 - r)
     second_move.wait()
     fetch(1 - r)
@@ -328,17 +343,47 @@
     batched(blocks, UNROLL, forward, send_part)
     total[spot] = partial[...]
 
-    def rest(b, comp):
+    def rest(b):
         left = w8 * (1.0 - jnp.exp(-d8 * (u[pl.ds(b, 1), :] * -1.0 + lengths_row(b) + ends[pl.ds(b, 1), :])))
         rem = jnp.sum(left, axis=0, keepdims=True)
-        remain[pl.ds(b, 1), :] = rem
-        return comp + two(jnp.broadcast_to(rem, (8, B)), rows[rows_at(b, B), :].astype(BF16))
+        return rem, two(jnp.broadcast_to(rem, (8, B)), rows[rows_at(b, B), :].astype(BF16))
 
     def lengths_row(b):
         return u[pl.ds(b, 1), B - 1 :]
 
-    comp = lax.fori_loop(0, blocks, rest, jnp.zeros((8, B), F32), unroll=4)
-
+    def summed(values):
+        while len(values) > 1:
+            values = [sum(values[i : i + 2]) for i in range(0, len(values), 2)]
+        return values[0]
+
+    def rests(g, comp):
+        found = [rest(g * UNROLL + i) for i in range(UNROLL)]
+        remain[rows_at(g, UNROLL), :] = jnp.concatenate([f[0] for f in found], 0)
+        return comp + summed([f[1] for f in found])
+
+    comp = lax.fori_loop(0, blocks // UNROLL, rests, jnp.zeros((8, B), F32))
+
+    row8 = iota((8, B), 0)
+
+    def thirds(a, places):
+        high, rest = halves(a)
+        mid, low = halves(rest)
+        out = jnp.zeros((8, B), F32)
+        for term, where in zip((high, mid, low), places):
+            for k in where:
+                out = jnp.where(row8 == k, term, out)
+        return out
+
+    xstack = thirds(xtot * (-1.0 / types), ((0, 2, 5), (1, 4), (3,)))
+    fill24 = jnp.zeros((B - 3 * width - 8, B), F32)
+
+    def prepare_turn(b):
+        lh, ll = halves(parted(w8 * jnp.exp(-d8 * (te[pl.ds(b, 1), :] - u[pl.ds(b, 1), :]))))
+        rstack = thirds(remain[pl.ds(b, 1), :], ((0, 1, 3), (2, 4), (5,)))
+        turn = jnp.concatenate([lh, lh, ll, rstack, fill24], 0).T.astype(BF16)
+        return [(lanes, (rows_at(b, B), slice(None)), turn)]
+
+    batched(blocks, UNROLL, prepare_turn)
     for g in range(blocks // UNROLL):
         for copy in part_copies(g):
             copy.wait()
@@ -358,17 +403,22 @@
     behind[2 * count :, :] = comp
     back_copies = share(behind, back, b_send, b_recv)
 
-    def spread(i, both):
-        b = r * shard_blocks + i
+    def spread(b):
         m = mark_row(b)
         hi, lo = lax.div(m, B), lax.rem(m, B)
         ih, il = halves(inverse[pl.ds(b, 1), :])
         wide = jnp.concatenate([jnp.broadcast_to(ih, (groups, B)), jnp.broadcast_to(il, (groups, B))], 0)
         left = jnp.where(lax.rem(iota((2 * groups, B), 0), groups) == hi, wide, 0.0).astype(BF16)
         right = (li == lo).astype(BF16)
+        return left, right
+
+    def spreads(g, both):
+        pairs = [spread(r * shard_blocks + g * 8 + i) for i in range(8)]
+        left = jnp.concatenate([p[0] for p in pairs], 1)
+        right = jnp.concatenate([p[1] for p in pairs], 1)
         return both + lax.dot_general(left, right, NT, preferred_element_type=F32)
 
-    both = lax.fori_loop(0, shard_blocks, spread, jnp.zeros((2 * groups, B), F32), unroll=2)
+    both = lax.fori_loop(0, shard_blocks // 8, spreads, jnp.zeros((2 * groups, B), F32))
     base_own[...] = (both[:groups] + both[groups:]).reshape(base_own.shape)
     base_copies = []
     for i, p in enumerate(peers):
@@ -407,55 +457,50 @@
             )
     recur(tuple(pending), True, False)
     events_all = blocks * B * half
-    minus[...] = jnp.where(lane < edge, comp_all * (1.0 / events_all), 0.0)
-
-    row8 = iota((8, B), 0)
-
-    def thirds(a, places):
-        high, rest = halves(a)
-        mid, low = halves(rest)
-        out = jnp.zeros((8, B), F32)
-        for term, where in zip((high, mid, low), places):
-            for k in where:
-                out = jnp.where(row8 == k, term, out)
-        return out
-
-    xstack = thirds(xtot * (-1.0 / types), ((0, 2, 5), (1, 4), (3,)))
-    fill24 = jnp.zeros((B - 3 * width - 8, B), F32)
-
-    def distant(b):
-        s = rows_at(b, B)
-        lh, ll = halves(parted(w8 * jnp.exp(-d8 * (te[pl.ds(b, 1), :] - u[pl.ds(b, 1), :]))))
-        rstack = thirds(remain[pl.ds(b, 1), :], ((0, 1, 3), (2, 4), (5,)))
-        turn = jnp.concatenate([lh, lh, ll, rstack, fill24], 0).T.astype(BF16)
-        sh, sl = halves(states[rows_at(b, width), :])
-        stack = jnp.concatenate([sh, sl, sh, xstack, fill24], 0)
-        value = dot(turn, jnp.where(lane < edge, 0.0, stack).astype(BF16))
-        return [(values, (s, slice(None)), inside[s, :] + value)]
-
-    def piece(g):
-        s = rows_at(g, UNROLL * B)
-        return pltpu.make_async_copy(values.at[s, :], values_out.at[s, :], out_sem.at[g])
-
-    batched(blocks, UNROLL, distant, lambda g: piece(g).start())
-
     for copy in base_copies:
         copy.wait()
     base_all = base_parts[0]
     for p in range(1, n):
         base_all = base_all + base_parts[p]
     grad_base[...] = base_all * (types / events_all) - t_end * (1.0 / events_all)
+    minus[...] = jnp.where(lane < edge, comp_all * (1.0 / events_all), 0.0)
+    finals = [
+        pltpu.make_async_copy(grad_base, base_out, end_sem.at[1]),
+        pltpu.make_async_copy(minus, minus_out, end_sem.at[2]),
+    ]
+    for copy in finals:
+        copy.start()
+
+    def distant(b):
+        s = rows_at(b, B)
+        sh, sl = halves(states[rows_at(b, width), :])
+        stack = jnp.concatenate([sh, sl, sh, xstack, fill24], 0)
+        value = dot(lanes[s, :], jnp.where(lane < edge, 0.0, stack).astype(BF16))
+        return [(values, (s, slice(None)), inside[s, :] + value)]
+
+    def piece(g):
+        s = rows_at(g, UNROLL * B)
+        return pltpu.make_async_copy(values.at[s, :], values_out.at[s, :], out_sem.at[g])
+
+    batched(blocks, UNROLL, distant, lambda g: piece(g).start())
+
     for copy in gathers:
         copy.wait_send()
+    for copy in finals + [marks_copy]:
+        copy.wait()
     for g in range(blocks // UNROLL):
         piece(g).wait()
 
 
-def scatter_kernel(marks, values_in, out, values, load_sem, out_sem, *tables):
+def scatter_kernel(marks_in, values_in, out, marks, values, load_sem, out_sem, *tables):
     count = len(tables)
     types = out.shape[0]
-    load = pltpu.make_async_copy(values_in, values, load_sem.at[0])
-    load.start()
+    loads = [
+        pltpu.make_async_copy(values_in, values, load_sem.at[0]),
+        pltpu.make_async_copy(marks_in, marks, load_sem.at[1]),
+    ]
+    for copy in loads:
+        copy.start()
 
     def zero(i, _):
         for t in tables:
@@ -463,7 +508,8 @@
         return 0
 
     lax.fori_loop(0, types // 32, zero, 0)
-    load.wait()
+    for copy in loads:
+        copy.wait()
     shards, blocks, _ = marks.shape
     for j in range(shards):
 
@@ -744,8 +790,8 @@
             jax.ShapeDtypeStruct((8, B), F32),
             jax.ShapeDtypeStruct((2, shard_blocks, B), jnp.int32),
         ],
-        in_specs=[SMEM, SMEM, VMEM, VMEM, HBM, HBM, VMEM],
-        out_specs=[HBM] + [VMEM] * 3,
+        in_specs=[HBM] * 7,
+        out_specs=[HBM] * 4,
         scratch_shapes=[
             pltpu.VMEM((B, types), BF16),
             pltpu.VMEM((types, B), F32),
@@ -771,6 +817,10 @@
             dma((half - 1,)), dma((half - 1,)),
             dma((n - 1,)), dma((n - 1,)),
             tall, dma((blocks // UNROLL,)),
+            pltpu.SMEM((count,), F32), pltpu.SMEM((count,), F32),
+            pltpu.VMEM((shard_blocks, B), jnp.int32), pltpu.VMEM((shard_blocks, B), jnp.int32),
+            pltpu.VMEM((groups, B), F32), pltpu.VMEM((groups // n, B), F32), pltpu.VMEM((8, B), F32),
+            pltpu.VMEM((2, shard_blocks, B), jnp.int32), dma((5,)), dma((3,)),
         ],
         compiler_params=pltpu.CompilerParams(
             collective_id=0, has_side_effects=True, vmem_limit_bytes=ALL_VMEM
@@ -781,9 +831,9 @@
     dense = pl.pallas_call(
         scatter_kernel,
         out_shape=jax.ShapeDtypeStruct((types, B), F32),
-        in_specs=[SMEM, HBM],
+        in_specs=[HBM] * 2,
         out_specs=HBM,
-        scratch_shapes=[tall, dma((1,)), dma((8,))] + [pltpu.VMEM((types, B), F32)] * 8,
+        scratch_shapes=[pltpu.SMEM((2, shard_blocks, B), jnp.int32), tall, dma((2,)), dma((8,))] + [pltpu.VMEM((types, B), F32)] * 8,
         compiler_params=pltpu.CompilerParams(vmem_limit_bytes=ALL_VMEM),
     )(marks_all, values)
 

time: 102 us -> 97.9 us (0.960)
  Pallas kernels: 99 us -> 94.8 us
    pallas_call x1, Pallas kernels: 44.2 us -> 42.6 us  [body(): pl.pallas_call(functools.partial(kernel, n, types / (events * half)), out...]
    pallas_call x1, Pallas kernels: 41 us -> 39.7 us  [body(): pl.pallas_call(functools.partial(front_kernel, n, lanes_n, rank), out_sha...]
    pallas_call x1, Pallas kernels: 13.7 us -> 12.6 us  [body(): pl.pallas_call(scatter_kernel, out_shape=jax.ShapeDtypeStruct((types, B),...]
where the time goes in v5:
time: 97.9 us; the launch traced here: 97.7 us
  Pallas kernels  94.8 us (97%)
  local copies, waits for them, and re-layouts  2.19 us (2%)
    pallas_call x1, Pallas kernels, body(): pl.pallas_call(functools.partial(kernel, n, types / (events * half)), out...  42.6 us
    pallas_call x1, Pallas kernels, body(): pl.pallas_call(functools.partial(front_kernel, n, lanes_n, rank), out_sha...  39.7 us
    pallas_call x1, Pallas kernels, body(): pl.pallas_call(scatter_kernel, out_shape=jax.ShapeDtypeStruct((types, B),...  12.6 us
    unnamed x7, local copies, waits for them, and re-layouts  2.19 us

profile of v5, /device:TPU:0, one launch (start us, length us, event | category | flops | bytes accessed | tf_op | source)
XLA Modules:
  0.0 97.7 jit_solution(1107067504567060243)
XLA Ops:
  0.6 39.7 %shard_map.94 = (f32[8192,128]{1,0:T(8,128)}, f32[8,128]{1,0:T(8,128)}, f32[8,128]{1,0:T(8,128)}, s32[2,32,128]{2,1,0:T(8,128)}) custom-call(f32[8]{0:T(128)} %weights_in.1, f32[8]{0:T(128)} %decay_in.1, s32[32,128]{1,0:T(8,128)} %bitcast.5, s32[32,128]{1,0:T(8,128)} %bitcast.6, bf16[128,8192]{1,0:T(8,128)(2,1)} %src.1, bf16[128,8192]{1,0:T(8,128)(2,1)} %exc.1, ...), custom_call_target="tpu_custom_call" | custom-call | tf_op jit(solution)/shard_map/pallas_call | solution.py:785
  40.3 0.0 copy-start
  40.3 12.6 %shard_map.95.source = f32[8192,128]{1,0:T(8,128)} custom-call(s32[2,32,128]{2,1,0:T(8,128)} %get-tuple-element.10.marks_in, f32[8192,128]{1,0:T(8,128)} %get-tuple-element.11.values_in), custom_call_target="tpu_custom_call" | custom-call | tf_op jit(solution)/shard_map/pallas_call | solution.py:831
  52.9 0.0 copy-done
  52.9 0.0 copy-start.1
  52.9 42.6 %shard_map.96 = (f32[128,1024]{1,0:T(8,128)S(1)}, f32[128,1024]{1,0:T(8,128)S(1)}) custom-call(f32[8,128]{1,0:T(8,128)S(1)} %copy-done, f32[8192,128]{1,0:T(8,128)} %shard_map.95.source), custom_call_target="tpu_custom_call" | custom-call | tf_op jit(solution)/shard_map/pallas_call | solution.py:858
  95.5 0.8 copy.13
  96.3 0.8 copy.14
  97.1 0.0 copy-done.1
  97.1 0.6 copy.15
Async XLA Ops:
  40.3 12.6 %copy-start = (f32[8,128]{1,0:T(8,128)S(1)}, f32[8,128]{1,0:T(8,128)}, u32[]{:S(2)}) copy-start(f32[8,128]{1,0:T(8,128)} %get-tuple-element.9.minus) | copy-start | bytes 12292
  52.9 44.2 %copy-start.1 = (f32[8,128]{1,0:T(8,128)S(1)}, f32[8,128]{1,0:T(8,128)}, u32[]{:S(2)}) copy-start(f32[8,128]{1,0:T(8,128)} %get-tuple-element.14) | copy-start | bytes 12292

commit v6 on v5

--- a/solution.py
+++ b/solution.py
@@ -233,7 +233,7 @@
                 pair = tuple(nxt)
             return pair
 
-        return lax.fori_loop(0, shard_blocks, step, start, unroll=2)
+        return lax.fori_loop(0, shard_blocks, step, start, unroll=8)
 
     def share(source, dest, send, recv):
         copies = []
@@ -288,7 +288,7 @@
             (base_e, (pl.ds(b, 1), slice(None)), jnp.sum(jnp.where(li == lo, found, 0.0), axis=0, keepdims=True)),
         ]
 
-    batched(blocks, UNROLL, within)
+    batched(blocks, 2 * UNROLL, within)
 
     for copy in state_copies:
         copy.wait()
@@ -383,7 +383,7 @@
         turn = jnp.concatenate([lh, lh, ll, rstack, fill24], 0).T.astype(BF16)
         return [(lanes, (rows_at(b, B), slice(None)), turn)]
 
-    batched(blocks, UNROLL, prepare_turn)
+    batched(blocks, 2 * UNROLL, prepare_turn)
     for g in range(blocks // UNROLL):
         for copy in part_copies(g):
             copy.wait()
@@ -396,7 +396,7 @@
         e8 = d8 * jnp.exp(-d8 * (u[pl.ds(b, 1), :] - ts[pl.ds(b, 1), :])) * inverse[pl.ds(b, 1), :]
         return [(sums, (rows_at(b, width), slice(None)), two(parted(e8), rows[rows_at(b, B), :].astype(BF16)))]
 
-    batched(blocks, UNROLL, reverse)
+    batched(blocks, 2 * UNROLL, reverse)
 
     for j, state in enumerate(recur((zero, zero), False, False)):
         behind[j * count : (j + 1) * count, :] = state
@@ -438,7 +438,7 @@
         both = dot(left, rows[s, :].astype(BF16))
         return [(inside, (s, slice(None)), jnp.where(lane < edge, excitation[s, :] * turned(ir), both[:B] + both[B:]))]
 
-    batched(blocks, UNROLL, feedback)
+    batched(blocks, 2 * UNROLL, feedback)
 
     for copy in back_copies:
         copy.wait()
@@ -507,7 +507,7 @@
             t[rows_at(i, 32), :] = jnp.zeros((32, B), F32)
         return 0
 
-    lax.fori_loop(0, types // 32, zero, 0)
+    lax.fori_loop(0, types // 32, zero, 0, unroll=4)
     for copy in loads:
         copy.wait()
     shards, blocks, _ = marks.shape
@@ -523,12 +523,13 @@
 
         lax.fori_loop(0, blocks, block, 0)
 
+    result = values if values.shape[0] >= types else tables[0]
     pieces = out_sem.shape[0]
     size = types // pieces
 
     def piece(c):
         s = rows_at(c, size)
-        return pltpu.make_async_copy(tables[0].at[s, :], out.at[s, :], out_sem.at[c])
+        return pltpu.make_async_copy(result.at[s, :], out.at[s, :], out_sem.at[c])
 
     def total(c, _):
         def add(i, _):
@@ -536,10 +537,10 @@
             acc = [t[s, :] for t in tables]
             while len(acc) > 1:
                 acc = [acc[i] + acc[i + 1] for i in range(0, len(acc), 2)]
-            tables[0][s, :] = acc[0]
+            result[s, :] = acc[0]
             return 0
 
-        lax.fori_loop(0, size // 32, add, 0, unroll=2)
+        lax.fori_loop(0, size // 32, add, 0, unroll=16)
         piece(c).start()
         return 0
 

time: 97.9 us -> 96 us (0.981)
  Pallas kernels: 94.8 us -> 92.9 us
    pallas_call x1, Pallas kernels: 12.6 us -> 11.6 us  [body(): pl.pallas_call(scatter_kernel, out_shape=jax.ShapeDtypeStruct((types, B),...]
where the time goes in v6:
time: 96 us; the launch traced here: 95.8 us
  Pallas kernels  92.9 us (97%)
  local copies, waits for them, and re-layouts  2.19 us (2%)
    pallas_call x1, Pallas kernels, body(): pl.pallas_call(functools.partial(kernel, n, types / (events * half)), out...  42.6 us
    pallas_call x1, Pallas kernels, body(): pl.pallas_call(functools.partial(front_kernel, n, lanes_n, rank), out_sha...  38.7 us
    pallas_call x1, Pallas kernels, body(): pl.pallas_call(scatter_kernel, out_shape=jax.ShapeDtypeStruct((types, B),...  11.6 us
    unnamed x7, local copies, waits for them, and re-layouts  2.19 us

profile of v6, /device:TPU:0, one launch (start us, length us, event | category | flops | bytes accessed | tf_op | source)
XLA Modules:
  0.0 95.8 jit_solution(4701794941565945118)
XLA Ops:
  0.6 38.7 %shard_map.94 = (f32[8192,128]{1,0:T(8,128)}, f32[8,128]{1,0:T(8,128)}, f32[8,128]{1,0:T(8,128)}, s32[2,32,128]{2,1,0:T(8,128)}) custom-call(f32[8]{0:T(128)} %weights_in.1, f32[8]{0:T(128)} %decay_in.1, s32[32,128]{1,0:T(8,128)} %bitcast.5, s32[32,128]{1,0:T(8,128)} %bitcast.6, bf16[128,8192]{1,0:T(8,128)(2,1)} %src.1, bf16[128,8192]{1,0:T(8,128)(2,1)} %exc.1, ...), custom_call_target="tpu_custom_call" | custom-call | tf_op jit(solution)/shard_map/pallas_call | solution.py:786
  39.4 0.0 copy-start
  39.4 11.6 %shard_map.95.source = f32[8192,128]{1,0:T(8,128)} custom-call(s32[2,32,128]{2,1,0:T(8,128)} %get-tuple-element.10.marks_in, f32[8192,128]{1,0:T(8,128)} %get-tuple-element.11.values_in), custom_call_target="tpu_custom_call" | custom-call | tf_op jit(solution)/shard_map/pallas_call | solution.py:832
  51.0 0.0 copy-done
  51.0 0.0 copy-start.1
  51.0 42.6 %shard_map.96 = (f32[128,1024]{1,0:T(8,128)S(1)}, f32[128,1024]{1,0:T(8,128)S(1)}) custom-call(f32[8,128]{1,0:T(8,128)S(1)} %copy-done, f32[8192,128]{1,0:T(8,128)} %shard_map.95.source), custom_call_target="tpu_custom_call" | custom-call | tf_op jit(solution)/shard_map/pallas_call | solution.py:859
  93.6 0.8 copy.13
  94.4 0.8 copy.14
  95.2 0.0 copy-done.1
  95.2 0.6 copy.15
Async XLA Ops:
  39.4 11.6 %copy-start = (f32[8,128]{1,0:T(8,128)S(1)}, f32[8,128]{1,0:T(8,128)}, u32[]{:S(2)}) copy-start(f32[8,128]{1,0:T(8,128)} %get-tuple-element.9.minus) | copy-start | bytes 12292
  51.0 44.2 %copy-start.1 = (f32[8,128]{1,0:T(8,128)S(1)}, f32[8,128]{1,0:T(8,128)}, u32[]{:S(2)}) copy-start(f32[8,128]{1,0:T(8,128)} %get-tuple-element.14) | copy-start | bytes 12292

commit v7 on v6

--- a/solution.py
+++ b/solution.py
@@ -206,7 +206,7 @@
     prepare(r)
     first_move.wait()
     fetch(r)
-    batched(shard_blocks, UNROLL, lambda b: emit(r * shard_blocks + b))
+    batched(shard_blocks, 2 * UNROLL, lambda b: emit(r * shard_blocks + b))
     for copy in gathers:
         copy.wait_recv()
     second_move = pltpu.make_async_copy(marks_out.at[1 - r], smarks.at[1 - r], mark_sem.at[1])
@@ -216,7 +216,7 @@
     prepare(1 - r)
     second_move.wait()
     fetch(1 - r)
-    batched(shard_blocks, UNROLL, lambda b: emit((1 - r) * shard_blocks + b))
+    batched(shard_blocks, 2 * UNROLL, lambda b: emit((1 - r) * shard_blocks + b))
 
     zero = jnp.zeros((count, B), F32)
 
@@ -357,11 +357,11 @@
         return values[0]
 
     def rests(g, comp):
-        found = [rest(g * UNROLL + i) for i in range(UNROLL)]
-        remain[rows_at(g, UNROLL), :] = jnp.concatenate([f[0] for f in found], 0)
+        found = [rest(g * 2 * UNROLL + i) for i in range(2 * UNROLL)]
+        remain[rows_at(g, 2 * UNROLL), :] = jnp.concatenate([f[0] for f in found], 0)
         return comp + summed([f[1] for f in found])
 
-    comp = lax.fori_loop(0, blocks // UNROLL, rests, jnp.zeros((8, B), F32))
+    comp = lax.fori_loop(0, blocks // (2 * UNROLL), rests, jnp.zeros((8, B), F32))
 
     row8 = iota((8, B), 0)
 
@@ -413,12 +413,12 @@
         return left, right
 
     def spreads(g, both):
-        pairs = [spread(r * shard_blocks + g * 8 + i) for i in range(8)]
+        pairs = [spread(r * shard_blocks + g * 16 + i) for i in range(16)]
         left = jnp.concatenate([p[0] for p in pairs], 1)
         right = jnp.concatenate([p[1] for p in pairs], 1)
         return both + lax.dot_general(left, right, NT, preferred_element_type=F32)
 
-    both = lax.fori_loop(0, shard_blocks // 8, spreads, jnp.zeros((2 * groups, B), F32))
+    both = lax.fori_loop(0, shard_blocks // 16, spreads, jnp.zeros((2 * groups, B), F32))
     base_own[...] = (both[:groups] + both[groups:]).reshape(base_own.shape)
     base_copies = []
     for i, p in enumerate(peers):

time: 96 us -> 95.5 us (level)
  no operation moved by 1% of the time
where the time goes in v7:
time: 95.5 us; the launch traced here: 95.2 us
  Pallas kernels  92.4 us (97%)
  local copies, waits for them, and re-layouts  2.19 us (2%)
    pallas_call x1, Pallas kernels, body(): pl.pallas_call(functools.partial(kernel, n, types / (events * half)), out...  42.6 us
    pallas_call x1, Pallas kernels, body(): pl.pallas_call(functools.partial(front_kernel, n, lanes_n, rank), out_sha...  38.2 us
    pallas_call x1, Pallas kernels, body(): pl.pallas_call(scatter_kernel, out_shape=jax.ShapeDtypeStruct((types, B),...  11.6 us
    unnamed x7, local copies, waits for them, and re-layouts  2.19 us

profile of v7, /device:TPU:0, one launch (start us, length us, event | category | flops | bytes accessed | tf_op | source)
XLA Modules:
  0.0 95.2 jit_solution(5932220934920749999)
XLA Ops:
  0.6 38.2 %shard_map.94 = (f32[8192,128]{1,0:T(8,128)}, f32[8,128]{1,0:T(8,128)}, f32[8,128]{1,0:T(8,128)}, s32[2,32,128]{2,1,0:T(8,128)}) custom-call(f32[8]{0:T(128)} %weights_in.1, f32[8]{0:T(128)} %decay_in.1, s32[32,128]{1,0:T(8,128)} %bitcast.5, s32[32,128]{1,0:T(8,128)} %bitcast.6, bf16[128,8192]{1,0:T(8,128)(2,1)} %src.1, bf16[128,8192]{1,0:T(8,128)(2,1)} %exc.1, ...), custom_call_target="tpu_custom_call" | custom-call | tf_op jit(solution)/shard_map/pallas_call | solution.py:786
  38.8 0.0 copy-start
  38.8 11.6 %shard_map.95.source = f32[8192,128]{1,0:T(8,128)} custom-call(s32[2,32,128]{2,1,0:T(8,128)} %get-tuple-element.10.marks_in, f32[8192,128]{1,0:T(8,128)} %get-tuple-element.11.values_in), custom_call_target="tpu_custom_call" | custom-call | tf_op jit(solution)/shard_map/pallas_call | solution.py:832
  50.4 0.0 copy-done
  50.4 0.0 copy-start.1
  50.4 42.6 %shard_map.96 = (f32[128,1024]{1,0:T(8,128)S(1)}, f32[128,1024]{1,0:T(8,128)S(1)}) custom-call(f32[8,128]{1,0:T(8,128)S(1)} %copy-done, f32[8192,128]{1,0:T(8,128)} %shard_map.95.source), custom_call_target="tpu_custom_call" | custom-call | tf_op jit(solution)/shard_map/pallas_call | solution.py:859
  93.0 0.8 copy.13
  93.8 0.8 copy.14
  94.6 0.0 copy-done.1
  94.6 0.6 copy.15
Async XLA Ops:
  38.8 11.6 %copy-start = (f32[8,128]{1,0:T(8,128)S(1)}, f32[8,128]{1,0:T(8,128)}, u32[]{:S(2)}) copy-start(f32[8,128]{1,0:T(8,128)} %get-tuple-element.9.minus) | copy-start | bytes 12292
  50.4 44.2 %copy-start.1 = (f32[8,128]{1,0:T(8,128)S(1)}, f32[8,128]{1,0:T(8,128)}, u32[]{:S(2)}) copy-start(f32[8,128]{1,0:T(8,128)} %get-tuple-element.14) | copy-start | bytes 12292
